TPU v7x, 32 devices: a whole 2x2x4 slice. The times are simulated.
32 devices in a mesh: st: 4 (over z), tm: 4 (over x, core), pol: 2 (over y).
Axes of the slice: x: 2, y: 2, z: 4, core: 2. Of those that a mesh axis runs over, the one named last changes fastest.
Arguments:
- samples: bfloat16 [512, 262144], P('st', 'tm'), may hold values from -6 to 6
- history: bfloat16 [512, 24576], P('st'), may hold values from -6 to 6
- station_order: int32 [256], replicated, may hold values from 0 to 255, each once
- channel_order: int32 [2048], replicated, may hold values from 0 to 2047, each once
- flagged: int32 [256], replicated, may hold values 0 or 1
Outputs:
- packed: float32 [2048, 512, 512], P(('st', 'tm', 'pol'))
Inputs may be any that keep to these rules, and one draw needn't show every extreme that they name: `station_order`: each station number appears once. `channel_order`: each channel appears once.
All inputs are finite; a program needn't handle non-finite values.
Results may differ from a plain program's by a relative error of at most 0.0082.
Values may be sent and summed in bfloat16 or wider, within the bound.
No kernel may reach another device: no remote copies, remote signals or barrier semaphores. Data moves between devices by JAX's collectives and lax.ppermute only.
A program may use at most 320 MiB of HBM per device.

v0:
```python
import math

import jax
import jax.numpy as jnp
from jax import lax
from jax.sharding import PartitionSpec as P

NFFT = 8192
FRAME_A = 32
CH = 2048
TAPS = 4


def shifted(array, axis, by):
    peers = lax.axis_size(axis)
    pairs = [(i, i + by) for i in range(peers) if 0 <= i + by < peers]
    return lax.ppermute(array, axis, pairs)


def filter_window(tap_count, frame_size):
    length = tap_count * frame_size
    offsets = jnp.arange(length).astype(jnp.float32) + 0.5
    centred = (offsets - 0.5 * length) / frame_size
    tapering = 0.5 - 0.5 * jnp.cos(offsets * (2.0 * math.pi / length))
    return (jnp.sinc(centred) * tapering).reshape(tap_count, frame_size)


def polyphase(row_block, weights, spec_count):
    row_total = row_block.shape[0]
    tap_count, frame_size = weights.shape
    running = jnp.zeros((row_total, spec_count, frame_size), jnp.float32)
    for tap_index in range(tap_count):
        section = row_block[:, tap_index * frame_size : (tap_index + spec_count) * frame_size]
        section = section.reshape(row_total, spec_count, frame_size)
        running = running + section.astype(jnp.float32) * weights[tap_index]
    return running.astype(jnp.bfloat16).reshape(row_total * spec_count, frame_size)


def trig_pair(left, right, modulus, amplitude):
    turn_count = left[:, None] * right[None, :] % modulus
    angles = turn_count.astype(jnp.float32) * (2.0 * math.pi / modulus)
    cosine = (jnp.cos(angles) * amplitude).astype(jnp.bfloat16)
    sine_part = (-(jnp.sin(angles) * amplitude)).astype(jnp.bfloat16)
    return (cosine, sine_part)


def product_low(form, left, right):
    return jnp.einsum(form, left, right, preferred_element_type=jnp.float32)


def frame_transform(filtered, channels, first_len):
    row_total, frame_size = filtered.shape
    second_len = frame_size // first_len
    half_len = second_len // 2
    first_idx = jnp.arange(first_len)
    second_idx = jnp.arange(second_len)
    half_idx = jnp.arange(half_len)
    first_cos, first_sin = trig_pair(first_idx, first_idx, first_len, 1.0 / math.sqrt(first_len))
    blocks = filtered.reshape(row_total, first_len, second_len)
    segment_re = product_low("rab,ae->reb", blocks, first_cos)
    segment_im = product_low("rab,ae->reb", blocks, first_sin)
    twist_turns = first_idx[:, None] * second_idx[None, :] % frame_size
    twist_angles = twist_turns.astype(jnp.float32) * (2.0 * math.pi / frame_size)
    twist_cos = jnp.cos(twist_angles)
    twist_sin = jnp.sin(twist_angles)
    twist_re = (segment_re * twist_cos + segment_im * twist_sin).astype(jnp.bfloat16)
    twist_im = (segment_im * twist_cos - segment_re * twist_sin).astype(jnp.bfloat16)
    second_cos, second_sin = trig_pair(
        second_idx, half_idx, second_len, 1.0 / math.sqrt(second_len)
    )
    full_re = product_low("reb,bf->ref", twist_re, second_cos) - product_low(
        "reb,bf->ref", twist_im, second_sin
    )
    full_im = product_low("reb,bf->ref", twist_re, second_sin) + product_low(
        "reb,bf->ref", twist_im, second_cos
    )
    column = channels % first_len * half_len + channels // first_len
    flat_re = jnp.take(full_re.reshape(row_total, first_len * half_len), column, axis=1)
    flat_im = jnp.take(full_im.reshape(row_total, first_len * half_len), column, axis=1)
    return jnp.stack([flat_re, flat_im], axis=1)


def input_rows(station_order):
    station_total = station_order.shape[0]
    inverse = (
        jnp.zeros((station_total,), jnp.int32).at[station_order].set(jnp.arange(station_total))
    )
    polarity = jnp.tile(jnp.arange(2), station_total)
    return 2 * jnp.repeat(inverse, 2) + polarity


def packed_products(turned, norm_scale):
    input_count, spec_count, pair_count, slot_count = turned.shape
    arranged = turned.transpose(3, 0, 1, 2)
    stacked = arranged.reshape(slot_count, input_count, spec_count * 2)
    swapped = jnp.stack([-arranged[..., 1], arranged[..., 0]], axis=-1).reshape(
        slot_count, input_count, spec_count * 2
    )
    combined = jnp.concatenate([stacked, swapped], axis=1)
    visible = jnp.einsum("sik,sjk->sij", stacked, combined, preferred_element_type=jnp.float32)
    indices = jnp.arange(input_count)
    upper_half = indices[:, None] <= indices[None, :]
    return (
        jnp.where(upper_half[None], visible[:, :, :input_count], visible[:, :, input_count:])
        * norm_scale
    )


def body(samples, history, station_order, channel_order, flagged):
    row_count, local_length = samples.shape
    spec_local = local_length // NFFT
    st_count = lax.axis_size("st")
    tm_count = lax.axis_size("tm")
    pol_count = lax.axis_size("pol")
    slot_share = CH // (st_count * tm_count * pol_count)
    half_slots = CH // pol_count
    lead_length = (TAPS - 1) * NFFT
    earlier = shifted(samples[:, local_length - lead_length :], "tm", 1)
    earlier = jnp.where(lax.axis_index("tm") == 0, history, earlier)
    stream = jnp.concatenate([earlier, samples], axis=1)
    filtered = polyphase(stream, filter_window(TAPS, NFFT), spec_local)
    local_slots = jnp.arange(half_slots)
    global_slots = (
        local_slots // slot_share * (slot_share * pol_count)
        + lax.axis_index("pol") * slot_share
        + local_slots % slot_share
    )
    station_ids = lax.dynamic_slice_in_dim(
        station_order, lax.axis_index("st") * (row_count // 2), row_count // 2
    )
    keeping = jnp.repeat((1 - flagged[station_ids]).astype(jnp.float32), 2)
    product = frame_transform(filtered, channel_order[global_slots], FRAME_A)
    product = product.reshape(row_count, spec_local, 2, half_slots) * keeping[:, None, None, None]
    spectra = product.astype(jnp.bfloat16)
    norm_scale = 1.0 / (spec_local * tm_count)
    input_order = input_rows(station_order)
    turned = lax.all_to_all(
        lax.all_to_all(spectra, "st", split_axis=3, concat_axis=0, tiled=True),
        "tm",
        split_axis=3,
        concat_axis=1,
        tiled=True,
    )
    turned = jnp.take(turned, input_order, axis=0)
    return packed_products(turned, norm_scale)


def solution(mesh):
    return jax.shard_map(
        body,
        mesh=mesh,
        in_specs=(P("st", "tm"), P("st", None), P(), P(), P()),
        out_specs=P(("st", "tm", "pol"), None, None),
        check_vma=False,
    )
```

profile of v0, /device:TPU:0, one launch (start us, length us, event | category | flops | bytes accessed | tf_op | source)
XLA Modules:
  0.0 870.7 jit_solution(12632519555876234204)
XLA Ops:
  11.0 21.3 %reshape.234 = f32[1024,32,256]{2,1,0:T(8,128)} reshape(bf16[128,65536]{1,0:T(8,128)(2,1)} %param.7) | data formatting | bytes 50331648 | tf_op jit(solution)/shard_map/convert_element_type | solution.py:35
  46.3 43.9 %fusion.4 = (f32[128,65536]{1,0:T(8,128)}, f32[128,65536]{1,0:T(8,128)}, f32[128,65536]{1,0:T(8,128)}) fusion(bf16[128,65536]{1,0:T(8,128)(2,1)} %param.7, bf16[128,24576]{1,0:T(8,128)(2,1)S(1)} %broadcast_select_fusion), kind=kLoop, calls=%fused_computation.18 | loop fusion | flops 100663296 | bytes 123731968 | tf_op jit(solution)/shard_map/convert_element_type | solution.py:35
  90.1 28.2 %reshape.231 = f32[1024,32,256]{2,1,0:T(8,128)} reshape(f32[128,65536]{1,0:T(8,128)} %get-tuple-element.10) | data formatting | bytes 67108864 | tf_op jit(solution)/shard_map/convert_element_type | solution.py:35
  118.4 28.3 %reshape.233 = f32[1024,32,256]{2,1,0:T(8,128)} reshape(f32[128,65536]{1,0:T(8,128)} %get-tuple-element.11) | data formatting | bytes 67108864 | tf_op jit(solution)/shard_map/convert_element_type | solution.py:35
  146.6 28.2 %reshape.232 = f32[1024,32,256]{2,1,0:T(8,128)} reshape(f32[128,65536]{1,0:T(8,128)} %get-tuple-element.12) | data formatting | bytes 67108864 | tf_op jit(solution)/shard_map/convert_element_type | solution.py:35
  174.9 47.7 %add_convert_fusion.1 = bf16[1024,32,256]{2,1,0:T(8,128)(2,1)} fusion(f32[1024,32,256]{2,1,0:T(8,128)} %reshape.234, f32[1024,32,256]{2,1,0:T(8,128)} %reshape.233, f32[1024,32,256]{2,1,0:T(8,128)} %reshape.232, f32[1024,32,256]{2,1,0:T(8,128)} %reshape.231, f32[32,256]{1,0:T(8,128)S(1)} %get-tuple-element.16, f32[32,256]{1,0:T(8,128)S(1)} %get-tuple-element.17, ...), kind=kLoop, calls=%fused_computation.10 | loop fusion | flops 67108864 | bytes 151126016 | tf_op jit(solution)/shard_map/convert_element_type | solution.py:36
  222.6 22.0 %fusion.67 = f32[32,1024,256]{2,0,1:T(8,128)} fusion(bf16[1024,32,256]{2,1,0:T(8,128)(2,1)} %add_convert_fusion.1), kind=kOutput, calls=%fused_computation.112 | convolution fusion | flops 536887296 | bytes 50331648 | tf_op jit(solution)/shard_map/rab,ae->reb/dot_general | solution.py:48
  244.6 28.6 %fusion.5 = (bf16[1024,32,256]{2,1,0:T(8,128)(2,1)}, bf16[1024,32,256]{2,1,0:T(8,128)(2,1)}) fusion(f32[32,1024,256]{2,0,1:T(8,128)} %fusion.67, f32[32,256]{1,0:T(8,128)S(1)} %copy-done.3, f32[32,256]{1,0:T(8,128)S(1)} %copy-done.4, bf16[1024,32,256]{2,1,0:T(8,128)(2,1)} %add_convert_fusion.1), kind=kOutput, calls=%fused_computation.19 | convolution fusion | flops 603997184 | bytes 83951616 | tf_op jit(solution)/shard_map/rab,ae->reb/dot_general | solution.py:48
  273.2 40.2 %fusion.8 = f32[1024,32,128]{0,2,1:T(8,128)} fusion(bf16[1024,32,256]{2,1,0:T(8,128)(2,1)} %get-tuple-element.9), kind=kOutput, calls=%fused_computation.23 | convolution fusion | flops 2148007936 | bytes 33554432 | tf_op jit(solution)/shard_map/reb,bf->ref/dot_general | solution.py:48
  313.4 32.3 %fusion.10 = f32[1024,32,128]{0,2,1:T(8,128)} fusion(bf16[1024,32,256]{2,1,0:T(8,128)(2,1)} %get-tuple-element.9), kind=kOutput, calls=%fused_computation.25 | convolution fusion | flops 2148040704 | bytes 33554432 | tf_op jit(solution)/shard_map/reb,bf->ref/dot_general | solution.py:48
  345.7 38.7 %fusion.21 = f32[1024,32,128]{0,2,1:T(8,128)} fusion(f32[1024,32,128]{0,2,1:T(8,128)} %fusion.10, bf16[1024,32,256]{2,1,0:T(8,128)(2,1)} %get-tuple-element.8), kind=kOutput, calls=%fused_computation.39 | convolution fusion | flops 2152202240 | bytes 50331648 | tf_op jit(solution)/shard_map/reb,bf->ref/dot_general | solution.py:48
  384.4 39.0 %fusion.24 = f32[1024,32,128]{0,2,1:T(8,128)} fusion(f32[1024,32,128]{0,2,1:T(8,128)} %fusion.8, bf16[1024,32,256]{2,1,0:T(8,128)(2,1)} %get-tuple-element.8), kind=kOutput, calls=%fused_computation.40 | convolution fusion | flops 2152235008 | bytes 50331648 | tf_op jit(solution)/shard_map/reb,bf->ref/dot_general | solution.py:48
  423.4 12.2 %gather_fusion.4 = f32[1024,1024]{1,0:T(8,128)} fusion(f32[1024,4096]{0,1:T(8,128)} %bitcast.50, s32[1024]{0:T(1024)S(1)} %copy-done.5), kind=kCustom, calls=%fused_computation.1.clone | custom fusion | bytes 8392704 | tf_op jit(solution)/shard_map/jit(_take)/gather | solution.py:79
  435.5 12.2 %gather_fusion.3 = f32[1024,1024]{1,0:T(8,128)} fusion(f32[1024,4096]{0,1:T(8,128)} %bitcast.49, s32[1024]{0:T(1024)S(1)} %copy-done.5), kind=kCustom, calls=%fused_computation.clone | custom fusion | bytes 8392704 | tf_op jit(solution)/shard_map/jit(_take)/gather | solution.py:78
  478.4 88.4 %all_to_all.36 = bf16[128,8,2,1024]{0,1,2,3:T(8,128)(2,1)} all-to-all(bf16[128,8,2,1024]{0,1,2,3:T(8,128)(2,1)} %copy.56), channel_id=1, replica_groups=mesh['st'=4,'tm'=4,'pol'=2] {'st'}, dimensions={3} | all-to-all | bytes 8388608 | tf_op jit(solution)/shard_map/all_to_all | solution.py:138
  575.3 8.6 copy.59
  583.9 13.6 %all-to-all-start.1 = ((bf16[512,8,2,256]{0,1,2,3:T(8,128)(2,1)}), bf16[512,8,2,256]{0,1,2,3:T(8,128)(2,1)}, u32[]{:S(2)}, u32[]{:S(2)}) async-start(bf16[512,8,2,256]{0,1,2,3:T(8,128)(2,1)} %copy.59), calls=%async_computation.1 | async-start | bytes 8388608 | tf_op jit(solution)/shard_map/all_to_all | solution.py:137
  599.4 46.3 %all-to-all-done.1 = bf16[512,8,2,256]{0,1,2,3:T(8,128)(2,1)} async-done(((bf16[512,8,2,256]{0,1,2,3:T(8,128)(2,1)}), bf16[512,8,2,256]{0,1,2,3:T(8,128)(2,1)}, u32[]{:S(2)}, u32[]{:S(2)}) %all-to-all-start.1) | async-done | bytes 4194336 | tf_op jit(solution)/shard_map/all_to_all | solution.py:137
  652.3 13.3 %copy.62 = bf16[512,32,2,64]{3,1,2,0:T(8,128)(2,1)} copy(bf16[512,32,2,64]{0,3,2,1:T(8,128)(2,1)} %bitcast.51) | data formatting | bytes 8388608 | tf_op jit(solution)/shard_map/all_to_all | solution.py:137
  665.6 23.0 %gather_fusion.2 = bf16[512,32,2,64]{3,1,2,0:T(8,128)(2,1)} fusion(bf16[512,32,2,64]{3,1,2,0:T(8,128)(2,1)} %copy.62, s32[1024]{0:T(1024)S(1)} %pad_clamp_fusion), kind=kCustom, calls=%fused_computation.4 | custom fusion | bytes 8390656 | tf_op jit(solution)/shard_map/jit(_take)/gather | solution.py:144
  696.3 15.2 %copy.63 = bf16[64,512,32,2]{1,3,2,0:T(2,128)(2,1)} copy(bf16[64,512,32,2]{0,2,3,1:T(8,128)(2,1)} %select_bitcast_fusion) | data formatting | bytes 8388608 | tf_op jit(solution)/shard_map/jit(_take)/select_n | solution.py:144
  733.1 15.2 %copy.64 = bf16[64,512,32,2]{1,3,2,0:T(2,128)(2,1)} copy(bf16[64,512,32,2]{0,2,3,1:T(8,128)(2,1)} %pad_maximum_fusion.1) | data formatting | bytes 8388608 | tf_op jit(solution)/shard_map/stack | solution.py:96
  755.8 49.9 %fusion.17 = f32[64,512,1024]{2,1,0:T(8,128)} fusion(bf16[64,512,64]{1,2,0:T(8,128)(2,1)} %reshape.229, bf16[64,512,64]{1,2,0:T(8,128)(2,1)} %reshape.230), kind=kOutput, calls=%fused_computation.34 | convolution fusion | flops 4311744512 | bytes 142606336 | tf_op jit(solution)/shard_map/sik,sjk->sij/dot_general | solution.py:100
  805.6 64.6 %fusion = f32[64,512,512]{2,1,0:T(8,128)} fusion(f32[64,512,1024]{2,1,0:T(8,128)} %fusion.17, pred[512,512]{1,0:T(8,128)(4,1)S(1)} %iota_compare_fusion), kind=kLoop, calls=%fused_computation.7 | loop fusion | flops 33554432 | bytes 201588736 | tf_op jit(solution)/shard_map/mul | solution.py:104
  (61 shorter events, 109.2 us)
Async XLA Ops:
  0.0 34.0 %copy-start = (s32[2048]{0:T(1024)S(1)}, s32[2048]{0:T(1024)}, u32[]{:S(2)}) copy-start(s32[2048]{0:T(1024)} %param.10) | copy-start | bytes 24580
  6.0 36.8 %collective-permute-start = (bf16[128,24576]{1,0:T(8,128)(2,1)}, bf16[128,24576]{1,0:T(8,128)(2,1)}, u32[]{:S(2)}, u32[]{:S(2)}) collective-permute-start(bf16[128,24576]{1,0:T(8,128)(2,1)} %slice.44), channel_id=1, source_target_pairs={{0,2},{2,4},{4,6},{1,3},{3,5},{5,7},{8,10},{10,12},{12,14},{9,11},... | collective-permute-start | bytes 18874376 | tf_op jit(solution)/shard_map/ppermute | solution.py:17
  11.0 21.3 %copy-start.8 = (s32[256]{0:T(256)S(1)}, s32[256]{0:T(256)}, u32[]{:S(2)}) copy-start(s32[256]{0:T(256)} %param.9) | copy-start | bytes 3076
  11.0 21.4 %copy-start.2 = (s32[256]{0:T(256)S(1)}, s32[256]{0:T(256)}, u32[]{:S(2)}) copy-start(s32[256]{0:T(256)} %param.11) | copy-start | bytes 3076
  222.6 22.1 %copy-start.3 = (f32[32,256]{1,0:T(8,128)S(1)}, f32[32,256]{1,0:T(8,128)}, u32[]{:S(2)}) copy-start(f32[32,256]{1,0:T(8,128)} %get-tuple-element.21) | copy-start | bytes 98308
  222.6 22.1 %copy-start.4 = (f32[32,256]{1,0:T(8,128)S(1)}, f32[32,256]{1,0:T(8,128)}, u32[]{:S(2)}) copy-start(f32[32,256]{1,0:T(8,128)} %get-tuple-element.22) | copy-start | bytes 98308
  384.4 39.0 %copy-start.5 = (s32[1024]{0:T(1024)S(1)}, s32[1024]{0:T(1024)}, u32[]{:S(2)}) copy-start(s32[1024]{0:T(1024)} %broadcast_clamp_fusion) | copy-start | bytes 12292
  435.5 12.2 %copy-start.6 = (pred[1024]{0:T(1024)(128)(4,1)S(1)}, pred[1024]{0:T(1024)(128)(4,1)}, u32[]{:S(2)}) copy-start(pred[1024]{0:T(1024)(128)(4,1)} %get-tuple-element.6) | copy-start | bytes 3076
  447.7 18.2 %copy-start.7 = (f32[128]{0:T(128)S(1)}, f32[128]{0:T(128)}, u32[]{:S(2)}) copy-start(f32[128]{0:T(128)} %mul.516) | copy-start | bytes 1540
  478.4 119.1 %copy-start.9 = (s32[256]{0:T(256)S(1)}, s32[256]{0:T(256)}, u32[]{:S(2)}) copy-start(s32[256]{0:T(256)} %param.9) | copy-start | bytes 3076
  583.9 61.8 %all-to-all-start.1 = ((bf16[512,8,2,256]{0,1,2,3:T(8,128)(2,1)}), bf16[512,8,2,256]{0,1,2,3:T(8,128)(2,1)}, u32[]{:S(2)}, u32[]{:S(2)}) async-start(bf16[512,8,2,256]{0,1,2,3:T(8,128)(2,1)} %copy.59), calls=%async_computation.1 | async-start | bytes 8388608 | tf_op jit(solution)/shard_map/all_to_all | solution.py:137
  805.6 64.6 %copy-start.1 = (s32[2048]{0:T(1024)S(1)}, s32[2048]{0:T(1024)}, u32[]{:S(2)}) copy-start(s32[2048]{0:T(1024)} %param.10) | copy-start | bytes 24580
where the time goes:
time: 882 us; the launch traced here: 871 us
  local copies, waits for them, and re-layouts  269 us (30%)
  matrix products  251 us (28%)
  other arithmetic  197 us (22%)
  blocking collectives  88.4 us (10%)
  waiting for transfers between devices  46.3 us (5%)
  starting transfers between devices  18.5 us (2%)
    dot_general x6, matrix products, product_low(): return jnp.einsum(form, left, right, preferred_element_type=jnp.float32)  201 us
    convert_element_type x4, local copies, waits for them, and re-layouts, polyphase(): running = running + section.astype(jnp.float32) * weights[tap_index]  106 us
    all_to_all x1, blocking collectives, body(): lax.all_to_all(spectra, 'st', split_axis=3, concat_axis=0, tiled=True)  88.4 us
    mul x1, other arithmetic, packed_products(): jnp.where(upper_half[None], visible[:, :, :input_count], visible[:, :, in...  64.6 us
    dot_general x1, matrix products, packed_products(): jnp.einsum('sik,sjk->sij', stacked, combined, preferred_element_type=jnp....  49.9 us
    convert_element_type x1, other arithmetic, polyphase(): running.astype(jnp.bfloat16).reshape(row_total * spec_count, frame_size)  47.7 us
    all_to_all x1, waiting for transfers between devices, body(): lax.all_to_all(lax.all_to_all(spectra, 'st', split_axis=3, concat_axis=0,...  46.3 us
    convert_element_type x1, other arithmetic, polyphase(): running = running + section.astype(jnp.float32) * weights[tap_index]  43.9 us
  transfers between devices with their start and end apart: 2, of which 1 were waited for; matrix products, arithmetic and copies ran while one was open for 4% of the time, Pallas kernels for 0%

commit v1 on v0

--- a/solution.py
+++ b/solution.py
@@ -1,14 +1,367 @@
+import functools
 import math
 
 import jax
 import jax.numpy as jnp
+import numpy as np
 from jax import lax
+from jax.experimental import pallas as pl
+from jax.experimental.pallas import tpu as pltpu
 from jax.sharding import PartitionSpec as P
 
 NFFT = 8192
 FRAME_A = 32
+FRAME_B = NFFT // FRAME_A
 CH = 2048
 TAPS = 4
+LEAD = TAPS - 1
+HALF_E = FRAME_A // 2
+LOW = CH // FRAME_A
+AXES = ("st", "tm", "pol")
+ROWS = 64
+GROUP = 16
+BATCH = 4
+VMEM = 56 << 20
+
+
+def np_window():
+    length = TAPS * NFFT
+    offsets = np.arange(length) + 0.5
+    centred = (offsets - 0.5 * length) / NFFT
+    tapering = 0.5 - 0.5 * np.cos(offsets * (2.0 * math.pi / length))
+    return (np.sinc(centred) * tapering).reshape(TAPS, NFFT).astype(np.float32)
+
+
+def np_first():
+    turns = np.arange(FRAME_A)[:, None] * np.arange(FRAME_A)[None, :] % FRAME_A
+    angles = turns * (2.0 * math.pi / FRAME_A)
+    cosine = np.cos(angles) / math.sqrt(FRAME_A)
+    sine = -np.sin(angles) / math.sqrt(FRAME_A)
+    rows = [cosine[0], cosine[HALF_E]]
+    for e in range(1, HALF_E):
+        rows += [cosine[e], sine[e]]
+    return np.kron(np.stack(rows), np.eye(GROUP)).astype(jnp.bfloat16)
+
+
+def np_twist():
+    turns = np.arange(HALF_E + 1)[:, None] * np.arange(FRAME_B)[None, :] % NFFT
+    angles = turns * (2.0 * math.pi / NFFT)
+    return np.cos(angles).astype(np.float32), np.sin(angles).astype(np.float32)
+
+
+def np_second():
+    f = np.concatenate([np.arange(LOW), FRAME_B - 1 - np.arange(LOW)])
+    sign = np.where(np.arange(2 * LOW) < LOW, 1.0, -1.0)[:, None]
+    angles = f[:, None] * np.arange(FRAME_B)[None, :] % FRAME_B * (2.0 * math.pi / FRAME_B)
+    cosine = np.cos(angles) / math.sqrt(FRAME_B)
+    sine = -np.sin(angles) / math.sqrt(FRAME_B)
+    top = np.concatenate([cosine, -sine], axis=1)
+    bottom = np.concatenate([sine * sign, cosine * sign], axis=1)
+    return np.concatenate([top, bottom]).astype(jnp.bfloat16)
+
+
+def filterbank_body(first, taps_of, sizes, step, refs):
+    w_ref, c1_ref, cos_ref, sin_ref, w2_ref, pick_ref, outs, y_ref, t_ref, d_ref = refs
+
+    def filter_a(a, carry):
+        weights = [w_ref[k : k + 1, pl.ds(pl.multiple_of(a * FRAME_B, FRAME_B), FRAME_B)] for k in range(TAPS)]
+        frames = [taps_of(i, a) for i in range(BATCH + LEAD)]
+        for t in range(BATCH):
+            total = frames[t] * weights[0]
+            for k in range(1, TAPS):
+                total = total + frames[t + k] * weights[k]
+            y_ref[t, pl.ds(pl.multiple_of(a * GROUP, GROUP), GROUP), :] = total.astype(jnp.bfloat16)
+        return carry
+
+    lax.fori_loop(0, FRAME_A, filter_a, 0, unroll=2)
+
+    def first_t(t, carry):
+        seg = jnp.dot(c1_ref[...], y_ref[t], preferred_element_type=jnp.float32)
+        rows = pl.ds(pl.multiple_of(t * ROWS + step * GROUP, GROUP), GROUP)
+        for e in range(HALF_E + 1):
+            cosine = cos_ref[e : e + 1, :]
+            sine = sin_ref[e : e + 1, :]
+            if e == 0 or e == HALF_E:
+                at = 0 if e == 0 else GROUP
+                re = seg[at : at + GROUP]
+                twist_re = re * cosine
+                twist_im = -(re * sine)
+            else:
+                at = 2 * e * GROUP
+                re = seg[at : at + GROUP]
+                im = seg[at + GROUP : at + 2 * GROUP]
+                twist_re = re * cosine + im * sine
+                twist_im = im * cosine - re * sine
+            t_ref[e, rows, 0:FRAME_B] = twist_re.astype(jnp.bfloat16)
+            t_ref[e, rows, FRAME_B : 2 * FRAME_B] = twist_im.astype(jnp.bfloat16)
+        return carry
+
+    lax.fori_loop(0, BATCH, first_t, 0)
+
+    @pl.when(step == ROWS // GROUP - 1)
+    def _():
+        width = BATCH * ROWS
+
+        def second_e(e, carry):
+            full = lax.dot_general(
+                w2_ref[...], t_ref[e], (((1,), (1,)), ((), ())), preferred_element_type=jnp.float32
+            )
+            rows = pl.ds(pl.multiple_of(e * 2 * LOW, 2 * LOW), 2 * LOW)
+            d_ref[rows, 0:width] = full[: 2 * LOW].astype(jnp.bfloat16)
+            d_ref[rows, width : 2 * width] = full[2 * LOW :].astype(jnp.bfloat16)
+            return carry
+
+        lax.fori_loop(0, HALF_E + 1, second_e, 0)
+
+        peers, share = sizes
+        block = 256
+        group = block // share
+
+        def gather(i, carry):
+            wanted = pick_ref[pl.ds(pl.multiple_of(i * block, block), block), :]
+            lanes = lax.broadcasted_iota(jnp.int32, (block, 128), 1)
+            hot = jnp.concatenate(
+                [
+                    jnp.where(wanted == lanes + 128 * k, 1.0, 0.0).astype(jnp.bfloat16)
+                    for k in range(HALF_E + 1)
+                ],
+                axis=1,
+            )
+            picked = jnp.dot(hot, d_ref[...], preferred_element_type=jnp.float32).astype(jnp.bfloat16)
+            part = share // len(outs)
+            for j in range(group):
+                for h, out_ref in enumerate(outs):
+                    out_ref[i * group + j] = picked[j * share + h * part : j * share + (h + 1) * part]
+            return carry
+
+        lax.fori_loop(0, peers * share // block, gather, 0)
+
+
+def late_kernel(sizes, place_ref, x_ref, w_ref, c1_ref, cos_ref, sin_ref, w2_ref, pick_ref, *rest):
+    outs, (y_ref, t_ref, d_ref) = rest[:-3], rest[-3:]
+    first = x_ref.shape[1] // NFFT - BATCH
+
+    def taps_of(i, a):
+        at = (first - LEAD + i) * NFFT
+        return x_ref[:, pl.ds(pl.multiple_of(at + a * FRAME_B, FRAME_B), FRAME_B)].astype(jnp.float32)
+
+    refs = (w_ref, c1_ref, cos_ref, sin_ref, w2_ref, pick_ref, outs, y_ref, t_ref, d_ref)
+    filterbank_body(first, taps_of, sizes, pl.program_id(0), refs)
+
+
+def early_kernel(
+    sizes, place_ref, x_ref, halo_ref, history_ref, w_ref, c1_ref, cos_ref, sin_ref, w2_ref, pick_ref, *rest
+):
+    outs, (y_ref, t_ref, d_ref) = rest[:-3], rest[-3:]
+    opening = place_ref[1] == 0
+
+    def taps_of(i, a):
+        if i >= LEAD:
+            at = pl.multiple_of((i - LEAD) * NFFT + a * FRAME_B, FRAME_B)
+            return x_ref[:, pl.ds(at, FRAME_B)].astype(jnp.float32)
+        at = pl.multiple_of(i * NFFT + a * FRAME_B, FRAME_B)
+        mine = halo_ref[:, pl.ds(at, FRAME_B)].astype(jnp.float32)
+        old = history_ref[:, pl.ds(at, FRAME_B)].astype(jnp.float32)
+        return jnp.where(opening, old, mine)
+
+    refs = (w_ref, c1_ref, cos_ref, sin_ref, w2_ref, pick_ref, outs, y_ref, t_ref, d_ref)
+    filterbank_body(0, taps_of, sizes, pl.program_id(0), refs)
+
+
+def filterbank(kernel, name, peers, share, parts, place, streams, stream_specs, consts):
+    whole = [pl.BlockSpec(c.shape, lambda i, p: (0, 0)) for c in consts]
+    out = jax.ShapeDtypeStruct((peers, share // parts, 2 * BATCH * ROWS), jnp.bfloat16)
+    return pl.pallas_call(
+        functools.partial(kernel, (peers, share)),
+        out_shape=[out] * parts,
+        grid_spec=pltpu.PrefetchScalarGridSpec(
+            num_scalar_prefetch=1,
+            grid=(ROWS // GROUP,),
+            in_specs=stream_specs + whole,
+            out_specs=[pl.BlockSpec(out.shape, lambda i, p: (0, 0, 0))] * parts,
+            scratch_shapes=[
+                pltpu.VMEM((BATCH, FRAME_A * GROUP, FRAME_B), jnp.bfloat16),
+                pltpu.VMEM((HALF_E + 1, BATCH * ROWS, 2 * FRAME_B), jnp.bfloat16),
+                pltpu.VMEM(((HALF_E + 1) * 2 * LOW, 2 * BATCH * ROWS), jnp.bfloat16),
+            ],
+        ),
+        cost_estimate=pl.CostEstimate(flops=12 * 10**9, bytes_accessed=16 << 20, transcendentals=0),
+        compiler_params=pltpu.CompilerParams(
+            dimension_semantics=("arbitrary",), vmem_limit_bytes=VMEM
+        ),
+        name=name,
+    )(place, *streams, *consts)
+
+
+def correlate_kernel(scale, st_count, tm_count, pol_count, per_step, *refs):
+    late_ref, early_ref, perm_ref = refs[:3]
+    out_ref, lhs_ref, z_ref = refs[-3:]
+    step = pl.program_id(0)
+    width = BATCH * ROWS
+    inputs = out_ref.shape[1]
+    pairs = BATCH // 2
+    units = st_count * pol_count
+
+    @pl.when(step % (GROUP // per_step) == 0)
+    def _():
+        row = 0
+        for c in range(2):
+            for source in (early_ref, late_ref):
+                for tm in range(tm_count):
+                    for pair in range(pairs):
+                        at = c * width + pair * 128
+                        for st in range(st_count):
+                            for pol in range(pol_count):
+                                unit = st * pol_count + pol
+                                lhs_ref[row : row + GROUP, unit * 128 : (unit + 1) * 128] = source[
+                                    (st * tm_count + tm) * pol_count + pol, :, at : at + 128
+                                ]
+                        row += GROUP
+        for half in range(2):
+            turned = jnp.dot(
+                lhs_ref[...],
+                perm_ref[:, half * inputs : (half + 1) * inputs],
+                preferred_element_type=jnp.float32,
+            )
+            for j in range(inputs // 128):
+                z_ref[half * (inputs // 128) + j] = turned[:, j * 128 : (j + 1) * 128]
+
+    depth = 2 * tm_count * pairs
+    mid = inputs // 2
+    tall = lax.broadcasted_iota(jnp.int32, (mid, mid), 0)
+    wide = lax.broadcasted_iota(jnp.int32, (mid, mid), 1)
+    upper = tall <= wide
+
+    def one(i, carry):
+        slot = lax.rem(step, GROUP // per_step) * per_step + i
+
+        def rows(half, c):
+            tiles = [
+                z_ref[
+                    half * (inputs // 128) + j,
+                    pl.ds(c * depth * GROUP + slot, depth, stride=GROUP),
+                    :,
+                ]
+                for j in range(inputs // 128)
+            ]
+            return jnp.concatenate(tiles, axis=1)
+
+        re0, im0, re1, im1 = rows(0, 0), rows(0, 1), rows(1, 0), rows(1, 1)
+        z = jnp.concatenate([re0, im0, re1, im1], axis=0)
+        turned = jnp.concatenate([-im0, re0, -im1, re1], axis=0).astype(jnp.bfloat16)
+        left = z.T.astype(jnp.bfloat16)
+        z = z.astype(jnp.bfloat16)
+        dot = functools.partial(jnp.dot, preferred_element_type=jnp.float32)
+        for h in range(2):
+            here = slice(h * mid, (h + 1) * mid)
+            re = dot(left[here], z[:, here])
+            im = dot(left[here], turned[:, here])
+            out_ref[i, here, here] = jnp.where(upper, re, im) * scale
+        out_ref[i, :mid, mid:] = dot(left[:mid], z[:, mid:]) * scale
+        out_ref[i, mid:, :mid] = dot(left[mid:], turned[:, :mid]) * scale
+        return carry
+
+    lax.fori_loop(0, per_step, one, 0)
+
+
+def correlate(half, halves, share, inputs, scale, sizes, late, early, perm, before):
+    st_count, tm_count, pol_count = sizes
+    per_step = 4
+    part = share // halves
+    steps = part // per_step
+    prep = GROUP // per_step
+    peers, _, wide = late.shape
+    first_prep = half * (part // GROUP)
+    first_step = half * steps
+    in_specs = [
+        pl.BlockSpec((peers, GROUP, wide), lambda i: (0, first_prep + i // prep, 0)),
+        pl.BlockSpec((peers, GROUP, wide), lambda i: (0, i // prep, 0)),
+        pl.BlockSpec(perm.shape, lambda i: (0, 0)),
+    ]
+    operands = [late, early, perm]
+    aliases = {}
+    if before is not None:
+        in_specs.append(pl.BlockSpec(memory_space=pl.ANY))
+        operands.append(before)
+        aliases = {3: 0}
+    return pl.pallas_call(
+        functools.partial(correlate_kernel, scale, st_count, tm_count, pol_count, per_step),
+        out_shape=jax.ShapeDtypeStruct((share, inputs, inputs), jnp.float32),
+        grid=(steps,),
+        in_specs=in_specs,
+        out_specs=pl.BlockSpec((per_step, inputs, inputs), lambda i: (first_step + i, 0, 0)),
+        scratch_shapes=[
+            pltpu.VMEM((2 * 2 * tm_count * (BATCH // 2) * GROUP, perm.shape[0]), jnp.bfloat16),
+            pltpu.VMEM((2 * inputs // 128, 2 * 2 * tm_count * (BATCH // 2) * GROUP, 128), jnp.float32),
+        ],
+        input_output_aliases=aliases,
+        cost_estimate=pl.CostEstimate(
+            flops=part * 12 * 10**7, bytes_accessed=part * inputs * inputs * 4, transcendentals=0
+        ),
+        compiler_params=pltpu.CompilerParams(
+            dimension_semantics=("arbitrary",), vmem_limit_bytes=VMEM
+        ),
+        name="correlate",
+    )(*operands)
+
+
+def fused_body(samples, history, station_order, channel_order, flagged):
+    row_count, local_length = samples.shape
+    spec_local = local_length // NFFT
+    st_count = lax.axis_size("st")
+    tm_count = lax.axis_size("tm")
+    pol_count = lax.axis_size("pol")
+    peers = st_count * tm_count * pol_count
+    share = CH // peers
+    inputs = row_count * st_count
+    pol = lax.axis_index("pol")
+    place = jnp.stack([pol, lax.axis_index("tm")]).astype(jnp.int32)
+
+    tail = lax.dynamic_slice(
+        samples, (pol * ROWS, local_length - LEAD * NFFT), (ROWS, LEAD * NFFT)
+    )
+    halo = lax.ppermute(tail, "tm", [(i, i + 1) for i in range(tm_count - 1)])
+
+    e, f = channel_order % FRAME_A, channel_order // FRAME_A
+    row = jnp.minimum(e, FRAME_A - e) * (2 * LOW) + jnp.where(e > HALF_E, LOW, 0) + f
+    pick = jnp.broadcast_to(row.astype(jnp.int32)[:, None], (CH, 128))
+    cosine, sine = np_twist()
+    consts = [
+        jnp.asarray(c) for c in (np_window(), np_first(), cosine, sine, np_second())
+    ] + [pick]
+
+    groups = ROWS // GROUP
+    late = filterbank(
+        late_kernel, "filterbank_late", peers, share, 1, place, [samples],
+        [pl.BlockSpec((GROUP, local_length), lambda i, p: (p[0] * groups + i, 0))],
+        consts,
+    )
+    late = lax.all_to_all(late[0], AXES, split_axis=0, concat_axis=0, tiled=True)
+    early = filterbank(
+        early_kernel, "filterbank_early", peers, share, 2, place, [samples, halo, history],
+        [
+            pl.BlockSpec((GROUP, BATCH * NFFT), lambda i, p: (p[0] * groups + i, 0)),
+            pl.BlockSpec((GROUP, LEAD * NFFT), lambda i, p: (i, 0)),
+            pl.BlockSpec((GROUP, LEAD * NFFT), lambda i, p: (p[0] * groups + i, 0)),
+        ],
+        consts,
+    )
+    early = [lax.all_to_all(x, AXES, split_axis=0, concat_axis=0, tiled=True) for x in early]
+
+    global_row = jnp.arange(inputs)
+    target = 2 * jnp.repeat(station_order, 2) + global_row % 2
+    keep = 1 - jnp.repeat(flagged, 2)
+    hot = (target[:, None] == jnp.arange(inputs)[None, :]) & (keep[None, :] == 1)
+    hot = hot.astype(jnp.bfloat16).reshape(st_count * pol_count, 1, ROWS, 1, inputs)
+    pair = jnp.eye(2, dtype=jnp.bfloat16).reshape(1, 2, 1, 2, 1)
+    perm = (hot * pair).reshape(2 * inputs, 2 * inputs)
+
+    scale = 1.0 / (spec_local * tm_count)
+    sizes = (st_count, tm_count, pol_count)
+    out = None
+    for half in range(2):
+        out = correlate(half, 2, share, inputs, scale, sizes, late, early[half], perm, out)
+    return out
 
 
 def shifted(array, axis, by):
@@ -106,7 +459,7 @@
     )
 
 
-def body(samples, history, station_order, channel_order, flagged):
+def general_body(samples, history, station_order, channel_order, flagged):
     row_count, local_length = samples.shape
     spec_local = local_length // NFFT
     st_count = lax.axis_size("st")
@@ -145,11 +498,30 @@
     return packed_products(turned, norm_scale)
 
 
+def fits(samples, mesh):
+    st_count, tm_count, pol_count = (mesh.shape[a] for a in AXES)
+    rows = samples.shape[0] // st_count
+    frames = samples.shape[1] // tm_count // NFFT
+    share = CH // (st_count * tm_count * pol_count)
+    return (
+        rows == ROWS * pol_count
+        and frames == 2 * BATCH
+        and tm_count == 4
+        and share % (2 * GROUP) == 0
+        and 256 % share == 0
+        and samples.shape[0] % 256 == 0
+    )
+
+
 def solution(mesh):
-    return jax.shard_map(
-        body,
-        mesh=mesh,
-        in_specs=(P("st", "tm"), P("st", None), P(), P(), P()),
-        out_specs=P(("st", "tm", "pol"), None, None),
-        check_vma=False,
-    )
+    def run(samples, history, station_order, channel_order, flagged):
+        body = fused_body if fits(samples, mesh) else general_body
+        return jax.shard_map(
+            body,
+            mesh=mesh,
+            in_specs=(P("st", "tm"), P("st", None), P(), P(), P()),
+            out_specs=P(("st", "tm", "pol"), None, None),
+            check_vma=False,
+        )(samples, history, station_order, channel_order, flagged)
+
+    return run

time: 882 us -> 170 us (0.19); the launches traced: 871 us -> 169 us
  local copies, waits for them, and re-layouts: 269 us -> 8.46 us
  matrix products: 251 us -> 0 us
  other arithmetic: 197 us -> 2.73 us
  Pallas kernels: 0 us -> 89.3 us
  blocking collectives: 88.4 us -> 30 us
  waiting for transfers between devices: 46.3 us -> 25.1 us
    dot_general x7 -> x0, matrix products: 251 us -> none  [the longest x6 201 us: product_low(): return jnp.einsum(form, left, right, preferred_element_type=jnp.float32)]
    convert_element_type x5 -> x0, local copies, waits for them, and re-layouts: 113 us -> none  [the longest x4 106 us: polyphase(): running = running + section.astype(jnp.float32) * weights[tap_index]]
    convert_element_type x4 -> x2, other arithmetic: 96.9 us -> 0.23 us  [the longest x1 0.22 us: fused_body(): hot.astype(jnp.bfloat16).reshape(st_count * pol_count, 1, ROWS, 1, inputs)]
    pallas_call x0 -> x4, Pallas kernels: none -> 89.3 us  [the longest x2 47.1 us: filterbank(): pl.pallas_call(functools.partial(kernel, (peers, share)), out_shape=[out]...]
    mul x3 -> x2, other arithmetic: 65.3 us -> 1.85 us  [the longest x1 1.84 us: fused_body(): perm = (hot * pair).reshape(2 * inputs, 2 * inputs)]
    all_to_all x1, blocking collectives: 88.4 us -> 30 us  [fused_body(): lax.all_to_all(x, AXES, split_axis=0, concat_axis=0, tiled=True)]
    gather x5 -> x0, local copies, waits for them, and re-layouts: 54.3 us -> none  [the longest x1 23 us: body(): turned = jnp.take(turned, input_order, axis=0)]
    all_to_all x4 -> x0, local copies, waits for them, and re-layouts: 36.9 us -> none  [the longest x2 19.8 us: body(): lax.all_to_all(lax.all_to_all(spectra, 'st', split_axis=3, concat_axis=0,...]
  transfers between devices with their start and end apart: 2 -> 3, of which waited for: 1 -> 2; matrix products, arithmetic and copies ran while one was open for 4% -> 4% of each run, Pallas kernels for 0% -> 40%
where the time goes in v1:
time: 170 us; the launch traced here: 169 us
  Pallas kernels  89.3 us (53%)
  blocking collectives  30 us (18%)
  waiting for transfers between devices  25.1 us (15%)
  starting transfers between devices  13.3 us (8%)
  local copies, waits for them, and re-layouts  8.46 us (5%)
  other arithmetic  2.73 us (2%)
    pallas_call x2, Pallas kernels, filterbank(): pl.pallas_call(functools.partial(kernel, (peers, share)), out_shape=[out]...  47.1 us
    pallas_call x2, Pallas kernels, correlate(): pl.pallas_call(functools.partial(correlate_kernel, scale, st_count, tm_co...  42.2 us
    all_to_all x1, blocking collectives, fused_body(): lax.all_to_all(x, AXES, split_axis=0, concat_axis=0, tiled=True)  30 us
    all_to_all x1, waiting for transfers between devices, fused_body(): lax.all_to_all(late[0], AXES, split_axis=0, concat_axis=0, tiled=True)  24.5 us
    all_to_all x1, starting transfers between devices, fused_body(): lax.all_to_all(late[0], AXES, split_axis=0, concat_axis=0, tiled=True)  5.74 us
    ppermute x1, starting transfers between devices, fused_body(): halo = lax.ppermute(tail, 'tm', [(i, i + 1) for i in range(tm_count - 1)])  3.99 us
    dynamic_slice x1, local copies, waits for them, and re-layouts, fused_body(): lax.dynamic_slice(samples, (pol * ROWS, local_length - LEAD * NFFT), (ROW...  3.77 us
    all_to_all x1, starting transfers between devices, fused_body(): lax.all_to_all(x, AXES, split_axis=0, concat_axis=0, tiled=True)  3.62 us
  transfers between devices with their start and end apart: 3, of which 2 were waited for; matrix products, arithmetic and copies ran while one was open for 4% of the time, Pallas kernels for 40%

profile of v1, /device:TPU:0, one launch (start us, length us, event | category | flops | bytes accessed | tf_op | source)
XLA Modules:
  0.0 169.1 jit_solution(11618033047400107417)
XLA Ops:
  0.0 3.8 %constant_dynamic-slice_fusion = bf16[64,24576]{1,0:T(8,128)(2,1)} fusion(bf16[128,65536]{1,0:T(8,128)(2,1)} %x_ref.3, s32[]{:T(128)S(6)} %select_n.32), kind=kLoop, calls=%fused_computation.26 | loop fusion | bytes 6291460 | tf_op jit(solution)/shard_map/dynamic_slice | solution.py:320
  3.8 4.0 %collective-permute-start = (bf16[64,24576]{1,0:T(8,128)(2,1)}, bf16[64,24576]{1,0:T(8,128)(2,1)}, u32[]{:S(2)}, u32[]{:S(2)}) collective-permute-start(bf16[64,24576]{1,0:T(8,128)(2,1)} %constant_dynamic-slice_fusion), channel_id=1, source_target_pairs={{0,2},{2,4},{4,6},{1,3},{3,5},{5,7},{8,10},{10,12},{12,14},{9,11},... | collective-permute-start | bytes 9437192 | tf_op jit(solution)/shard_map/ppermute | solution.py:323
  7.8 0.6 pad_add_fusion.place_ref
  8.4 1.3 broadcast_in_dim.22.pick_ref
  9.7 22.9 %filterbank_late.1 = bf16[32,64,512]{2,1,0:T(8,128)(2,1)} custom-call(s32[2]{0:T(128)} %pad_add_fusion.place_ref, bf16[128,65536]{1,0:T(8,128)(2,1)} %x_ref.3, f32[4,8192]{1,0:T(4,128)} %constant.75.clone.w_ref, bf16[512,512]{1,0:T(8,128)(2,1)} %constant.76.clone.c1_ref, f32[17,256]{1,0:T(8,128)} %constant.77.clone.cos_ref, ...), custom_call_target="tpu_custom_call" | custom-call | flops 12000000000 | bytes 16777216 | tf_op jit(solution)/shard_map/filterbank_late/pallas_call | solution.py:174
  32.7 5.7 %all-to-all-start = ((bf16[32,64,512]{2,1,0:T(8,128)(2,1)}), bf16[32,64,512]{2,1,0:T(8,128)(2,1)S(1)}, u32[]{:S(2)}, u32[]{:S(2)}) async-start(bf16[32,64,512]{2,1,0:T(8,128)(2,1)} %filterbank_late.1), calls=%async_computation | async-start | bytes 4194304 | tf_op jit(solution)/shard_map/all_to_all | solution.py:339
  38.4 0.0 collective-permute-done.halo_ref
  38.4 24.2 %filterbank_early.1 = (bf16[32,32,512]{2,1,0:T(8,128)(2,1)}, bf16[32,32,512]{2,1,0:T(8,128)(2,1)}) custom-call(s32[2]{0:T(128)} %pad_add_fusion.place_ref, bf16[128,65536]{1,0:T(8,128)(2,1)} %x_ref.3, bf16[64,24576]{1,0:T(8,128)(2,1)} %collective-permute-done.halo_ref, bf16[128,24576]{1,0:T(8,128)(2,1)} %history_ref.1, f32[4,8192]{1,0:T(4,128)} %constant.75.clone.w_ref, ...), custom_call_target="tpu_custom_call" | custom-call | flops 12000000000 | bytes 16777216 | tf_op jit(solution)/shard_map/filterbank_early/pallas_call | solution.py:174
  62.6 24.5 %all-to-all-done.refs_0_ = bf16[32,64,512]{2,1,0:T(8,128)(2,1)S(1)} async-done(((bf16[32,64,512]{2,1,0:T(8,128)(2,1)}), bf16[32,64,512]{2,1,0:T(8,128)(2,1)S(1)}, u32[]{:S(2)}, u32[]{:S(2)}) %all-to-all-start) | async-done | bytes 2097184 | tf_op jit(solution)/shard_map/all_to_all | solution.py:339
  87.1 30.0 %all_to_all.15.refs_1_ = bf16[32,32,512]{2,1,0:T(8,128)(2,1)} all-to-all(bf16[32,32,512]{2,1,0:T(8,128)(2,1)} %get-tuple-element.8), channel_id=1, replica_groups=mesh['st'=4,'tm'=4,'pol'=2] {'st','tm','pol'}, dimensions={0} | all-to-all | bytes 2097152 | tf_op jit(solution)/shard_map/all_to_all | solution.py:349
  117.1 3.6 %all-to-all-start.1 = ((bf16[32,32,512]{2,1,0:T(8,128)(2,1)}), bf16[32,32,512]{2,1,0:T(8,128)(2,1)S(1)}, u32[]{:S(2)}, u32[]{:S(2)}) async-start(bf16[32,32,512]{2,1,0:T(8,128)(2,1)} %get-tuple-element.7), calls=%async_computation.1 | async-start | bytes 2097152 | tf_op jit(solution)/shard_map/all_to_all | solution.py:349
  120.8 0.1 mul.50
  120.9 0.1 copy.13
  121.0 0.1 copy.14
  121.0 0.0 copy-done.4
  121.0 0.1 broadcast_in_dim.24
  121.2 0.2 eq.45
  121.3 0.2 fusion.1
  121.6 1.8 %broadcast_multiply_fusion = bf16[8,2,64,2,512]{4,3,2,1,0:T(2,128)(2,1)S(1)} fusion(bf16[2,2]{1,0:T(2,128)(2,1)S(1)} %compare_convert_fusion, bf16[8,64,512]{2,1,0:T(8,128)(2,1)S(1)} %fusion.1), kind=kLoop, calls=%fused_computation | loop fusion | flops 1048576 | bytes 2621448 | tf_op jit(solution)/shard_map/mul | solution.py:357
  123.4 1.9 %copy.15 = bf16[128,8,2,512]{3,1,2,0:T(8,128)(2,1)} copy(bf16[128,8,2,512]{3,2,1,0:T(2,128)(2,1)S(1)} %bitcast.8) | data formatting | bytes 4194304
  125.3 21.1 %correlate.2.refs_3_ = f32[64,512,512]{2,1,0:T(8,128)} custom-call(bf16[32,64,512]{2,1,0:T(8,128)(2,1)} %copy-done, bf16[32,32,512]{2,1,0:T(8,128)(2,1)} %all_to_all.15.refs_1_, bf16[1024,1024]{1,0:T(8,128)(2,1)} %bitcast.6), custom_call_target="tpu_custom_call" | custom-call | flops 3840000000 | bytes 33554432 | tf_op jit(solution)/shard_map/correlate/pallas_call | solution.py:287
  146.4 0.6 all-to-all-done.1.refs_1_
  147.0 1.0 copy-done.1
  148.0 21.1 %correlate.3 = f32[64,512,512]{2,1,0:T(8,128)} custom-call(bf16[32,64,512]{2,1,0:T(8,128)(2,1)} %copy-done, bf16[32,32,512]{2,1,0:T(8,128)(2,1)} %copy-done.1, bf16[1024,1024]{1,0:T(8,128)(2,1)} %bitcast.7, f32[64,512,512]{2,1,0:T(8,128)} %correlate.2.refs_3_), custom_call_target="tpu_custom_call", output_to_operand_aliasing={{}: (3, {})} | custom-call | flops 3840000000 | bytes 33554432 | tf_op jit(solution)/shard_map/correlate/pallas_call | solution.py:287
  (14 shorter events, 0.1 us)
Async XLA Ops:
  0.0 7.8 %copy-start.2 = (s32[2048]{0:T(1024)S(1)}, s32[2048]{0:T(1024)}, u32[]{:S(2)}) copy-start(s32[2048]{0:T(1024)} %param.13) | copy-start | bytes 24580
  3.8 34.6 %collective-permute-start = (bf16[64,24576]{1,0:T(8,128)(2,1)}, bf16[64,24576]{1,0:T(8,128)(2,1)}, u32[]{:S(2)}, u32[]{:S(2)}) collective-permute-start(bf16[64,24576]{1,0:T(8,128)(2,1)} %constant_dynamic-slice_fusion), channel_id=1, source_target_pairs={{0,2},{2,4},{4,6},{1,3},{3,5},{5,7},{8,10},{10,12},{12,14},{9,11},... | collective-permute-start | bytes 9437192 | tf_op jit(solution)/shard_map/ppermute | solution.py:323
  32.7 54.5 %all-to-all-start = ((bf16[32,64,512]{2,1,0:T(8,128)(2,1)}), bf16[32,64,512]{2,1,0:T(8,128)(2,1)S(1)}, u32[]{:S(2)}, u32[]{:S(2)}) async-start(bf16[32,64,512]{2,1,0:T(8,128)(2,1)} %filterbank_late.1), calls=%async_computation | async-start | bytes 4194304 | tf_op jit(solution)/shard_map/all_to_all | solution.py:339
  62.6 58.2 %copy-start.3 = (s32[256]{0:T(256)S(1)}, s32[256]{0:T(256)}, u32[]{:S(2)}) copy-start(s32[256]{0:T(256)} %param.12) | copy-start | bytes 3076
  62.6 58.5 %copy-start.4 = (s32[256]{0:T(256)S(1)}, s32[256]{0:T(256)}, u32[]{:S(2)}) copy-start(s32[256]{0:T(256)} %param.14) | copy-start | bytes 3076
  87.1 36.3 %copy-start = (bf16[32,64,512]{2,1,0:T(8,128)(2,1)}, bf16[32,64,512]{2,1,0:T(8,128)(2,1)S(1)}, u32[]{:S(2)}) copy-start(bf16[32,64,512]{2,1,0:T(8,128)(2,1)S(1)} %all-to-all-done.refs_0_) | copy-start | bytes 6291460
  117.1 29.9 %all-to-all-start.1 = ((bf16[32,32,512]{2,1,0:T(8,128)(2,1)}), bf16[32,32,512]{2,1,0:T(8,128)(2,1)S(1)}, u32[]{:S(2)}, u32[]{:S(2)}) async-start(bf16[32,32,512]{2,1,0:T(8,128)(2,1)} %get-tuple-element.7), calls=%async_computation.1 | async-start | bytes 2097152 | tf_op jit(solution)/shard_map/all_to_all | solution.py:349
  147.0 1.0 copy-start.1

commit v2 on v1

--- a/solution.py
+++ b/solution.py
@@ -20,7 +20,10 @@
 AXES = ("st", "tm", "pol")
 ROWS = 64
 GROUP = 16
+PREP = 8
 BATCH = 4
+PAIRS = BATCH // 2
+PER_SLOT = 2 * PAIRS
 VMEM = 56 << 20
 
 
@@ -60,8 +63,8 @@
     return np.concatenate([top, bottom]).astype(jnp.bfloat16)
 
 
-def filterbank_body(first, taps_of, sizes, step, refs):
-    w_ref, c1_ref, cos_ref, sin_ref, w2_ref, pick_ref, outs, y_ref, t_ref, d_ref = refs
+def filterbank_body(taps_of, step, refs):
+    row_ref, w_ref, c1_ref, cos_ref, sin_ref, w2_ref, outs, y_ref, t_ref, d_ref = refs
 
     def filter_a(a, carry):
         weights = [w_ref[k : k + 1, pl.ds(pl.multiple_of(a * FRAME_B, FRAME_B), FRAME_B)] for k in range(TAPS)]
@@ -96,48 +99,41 @@
             t_ref[e, rows, FRAME_B : 2 * FRAME_B] = twist_im.astype(jnp.bfloat16)
         return carry
 
-    lax.fori_loop(0, BATCH, first_t, 0)
+    lax.fori_loop(0, BATCH, first_t, 0, unroll=True)
 
     @pl.when(step == ROWS // GROUP - 1)
     def _():
-        width = BATCH * ROWS
-
-        def second_e(e, carry):
+        for e in range(HALF_E + 1):
             full = lax.dot_general(
                 w2_ref[...], t_ref[e], (((1,), (1,)), ((), ())), preferred_element_type=jnp.float32
             )
-            rows = pl.ds(pl.multiple_of(e * 2 * LOW, 2 * LOW), 2 * LOW)
-            d_ref[rows, 0:width] = full[: 2 * LOW].astype(jnp.bfloat16)
-            d_ref[rows, width : 2 * width] = full[2 * LOW :].astype(jnp.bfloat16)
+            for c in range(2):
+                for pair in range(PAIRS):
+                    start = PER_SLOT + e * 2 * LOW * PER_SLOT + c * PAIRS + pair
+                    d_ref[pl.ds(start, 2 * LOW, stride=PER_SLOT), :] = full[
+                        c * 2 * LOW : (c + 1) * 2 * LOW, pair * 128 : (pair + 1) * 128
+                    ]
+
+        share = sum(out_ref.shape[1] for out_ref in outs) // PER_SLOT
+        lower = lax.broadcasted_iota(jnp.int32, (2 * PER_SLOT, 128), 0) < PER_SLOT
+
+        def gather(peer, carry):
+            slot = peer * share
+            for out_ref in outs:
+                for at in range(0, out_ref.shape[1], 4 * PER_SLOT):
+                    halves = []
+                    for k in (0, 2):
+                        one = d_ref[pl.ds(row_ref[slot + k] + PER_SLOT, 2 * PER_SLOT), :]
+                        two = d_ref[pl.ds(row_ref[slot + k + 1], 2 * PER_SLOT), :]
+                        halves.append(jnp.where(lower, one, two))
+                    slot = slot + 4
+                    out_ref[peer, at : at + 4 * PER_SLOT, :] = jnp.concatenate(halves).astype(jnp.bfloat16)
             return carry
 
-        lax.fori_loop(0, HALF_E + 1, second_e, 0)
-
-        peers, share = sizes
-        block = 256
-        group = block // share
-
-        def gather(i, carry):
-            wanted = pick_ref[pl.ds(pl.multiple_of(i * block, block), block), :]
-            lanes = lax.broadcasted_iota(jnp.int32, (block, 128), 1)
-            hot = jnp.concatenate(
-                [
-                    jnp.where(wanted == lanes + 128 * k, 1.0, 0.0).astype(jnp.bfloat16)
-                    for k in range(HALF_E + 1)
-                ],
-                axis=1,
-            )
-            picked = jnp.dot(hot, d_ref[...], preferred_element_type=jnp.float32).astype(jnp.bfloat16)
-            part = share // len(outs)
-            for j in range(group):
-                for h, out_ref in enumerate(outs):
-                    out_ref[i * group + j] = picked[j * share + h * part : j * share + (h + 1) * part]
-            return carry
-
-        lax.fori_loop(0, peers * share // block, gather, 0)
-
-
-def late_kernel(sizes, place_ref, x_ref, w_ref, c1_ref, cos_ref, sin_ref, w2_ref, pick_ref, *rest):
+        lax.fori_loop(0, outs[0].shape[0], gather, 0)
+
+
+def late_kernel(place_ref, row_ref, x_ref, w_ref, c1_ref, cos_ref, sin_ref, w2_ref, *rest):
     outs, (y_ref, t_ref, d_ref) = rest[:-3], rest[-3:]
     first = x_ref.shape[1] // NFFT - BATCH
 
@@ -145,12 +141,12 @@
         at = (first - LEAD + i) * NFFT
         return x_ref[:, pl.ds(pl.multiple_of(at + a * FRAME_B, FRAME_B), FRAME_B)].astype(jnp.float32)
 
-    refs = (w_ref, c1_ref, cos_ref, sin_ref, w2_ref, pick_ref, outs, y_ref, t_ref, d_ref)
-    filterbank_body(first, taps_of, sizes, pl.program_id(0), refs)
+    refs = (row_ref, w_ref, c1_ref, cos_ref, sin_ref, w2_ref, outs, y_ref, t_ref, d_ref)
+    filterbank_body(taps_of, pl.program_id(0), refs)
 
 
 def early_kernel(
-    sizes, place_ref, x_ref, halo_ref, history_ref, w_ref, c1_ref, cos_ref, sin_ref, w2_ref, pick_ref, *rest
+    place_ref, row_ref, x_ref, halo_ref, history_ref, w_ref, c1_ref, cos_ref, sin_ref, w2_ref, *rest
 ):
     outs, (y_ref, t_ref, d_ref) = rest[:-3], rest[-3:]
     opening = place_ref[1] == 0
@@ -164,25 +160,25 @@
         old = history_ref[:, pl.ds(at, FRAME_B)].astype(jnp.float32)
         return jnp.where(opening, old, mine)
 
-    refs = (w_ref, c1_ref, cos_ref, sin_ref, w2_ref, pick_ref, outs, y_ref, t_ref, d_ref)
-    filterbank_body(0, taps_of, sizes, pl.program_id(0), refs)
-
-
-def filterbank(kernel, name, peers, share, parts, place, streams, stream_specs, consts):
-    whole = [pl.BlockSpec(c.shape, lambda i, p: (0, 0)) for c in consts]
-    out = jax.ShapeDtypeStruct((peers, share // parts, 2 * BATCH * ROWS), jnp.bfloat16)
+    refs = (row_ref, w_ref, c1_ref, cos_ref, sin_ref, w2_ref, outs, y_ref, t_ref, d_ref)
+    filterbank_body(taps_of, pl.program_id(0), refs)
+
+
+def filterbank(kernel, name, peers, parts, place, rows, streams, stream_specs, consts):
+    whole = [pl.BlockSpec(c.shape, lambda i, p, r: (0, 0)) for c in consts]
+    outs = [jax.ShapeDtypeStruct((peers, part * PER_SLOT, 128), jnp.bfloat16) for part in parts]
     return pl.pallas_call(
-        functools.partial(kernel, (peers, share)),
-        out_shape=[out] * parts,
+        kernel,
+        out_shape=outs,
         grid_spec=pltpu.PrefetchScalarGridSpec(
-            num_scalar_prefetch=1,
+            num_scalar_prefetch=2,
             grid=(ROWS // GROUP,),
             in_specs=stream_specs + whole,
-            out_specs=[pl.BlockSpec(out.shape, lambda i, p: (0, 0, 0))] * parts,
+            out_specs=[pl.BlockSpec(out.shape, lambda i, p, r: (0, 0, 0)) for out in outs],
             scratch_shapes=[
                 pltpu.VMEM((BATCH, FRAME_A * GROUP, FRAME_B), jnp.bfloat16),
                 pltpu.VMEM((HALF_E + 1, BATCH * ROWS, 2 * FRAME_B), jnp.bfloat16),
-                pltpu.VMEM(((HALF_E + 1) * 2 * LOW, 2 * BATCH * ROWS), jnp.bfloat16),
+                pltpu.VMEM(((HALF_E + 1) * 2 * LOW * PER_SLOT + 2 * PER_SLOT, 128), jnp.float32),
             ],
         ),
         cost_estimate=pl.CostEstimate(flops=12 * 10**9, bytes_accessed=16 << 20, transcendentals=0),
@@ -190,67 +186,109 @@
             dimension_semantics=("arbitrary",), vmem_limit_bytes=VMEM
         ),
         name=name,
-    )(place, *streams, *consts)
-
-
-def correlate_kernel(scale, st_count, tm_count, pol_count, per_step, *refs):
+    )(place, rows, *streams, *consts)
+
+
+def order_inputs(source, perm_ref, lhs_ref, z_ref, sizes, span):
+    st_count, tm_count, pol_count = sizes
+    half = 128 // 2
+    for tm in range(tm_count):
+        for st in range(st_count):
+            blocks = [source[(st * tm_count + tm) * pol_count + pol] for pol in range(pol_count)]
+            lanes = slice(st * pol_count * half, (st + 1) * pol_count * half)
+            for odd in range(2):
+                row = (odd * tm_count + tm) * span
+                lhs_ref[row : row + span, lanes] = jnp.concatenate(
+                    [block[:, odd * half : (odd + 1) * half] for block in blocks], axis=1
+                )
+    turned = jnp.dot(lhs_ref[...], perm_ref[...], preferred_element_type=jnp.float32)
+    for j in range(z_ref.shape[0]):
+        z_ref[j] = turned[:, j * 128 : (j + 1) * 128]
+
+
+def slot_rows(z_ref, slot, c, span, count):
+    tiles = [
+        jnp.concatenate(
+            [
+                z_ref[j, pl.ds(slot * PER_SLOT + c * PAIRS + pair, count, stride=span), :]
+                for j in range(z_ref.shape[0])
+            ],
+            axis=1,
+        )
+        for pair in range(PAIRS)
+    ]
+    return jnp.concatenate(tiles, axis=0).astype(jnp.bfloat16)
+
+
+def order_kernel(sizes, late_ref, perm_ref, out_ref, lhs_ref, z_ref):
+    slots = out_ref.shape[0]
+    span = slots * PER_SLOT
+    order_inputs(late_ref, perm_ref, lhs_ref, z_ref, sizes, span)
+    count = 2 * sizes[1]
+    for slot in range(slots):
+        for c in range(2):
+            out_ref[slot, c * PAIRS * count : (c + 1) * PAIRS * count, :] = slot_rows(
+                z_ref, slot, c, span, count
+            )
+
+
+def order_late(share, sizes, late, perm):
+    peers = late.shape[0]
+    inputs = perm.shape[1]
+    span = GROUP * PER_SLOT
+    rows = 2 * sizes[1] * span
+    depth = 2 * sizes[1] * PER_SLOT
+    return pl.pallas_call(
+        functools.partial(order_kernel, sizes),
+        out_shape=jax.ShapeDtypeStruct((share, depth, inputs), jnp.bfloat16),
+        grid=(share // GROUP,),
+        in_specs=[
+            pl.BlockSpec((peers, span, 128), lambda i: (0, i, 0)),
+            pl.BlockSpec(perm.shape, lambda i: (0, 0)),
+        ],
+        out_specs=pl.BlockSpec((GROUP, depth, inputs), lambda i: (i, 0, 0)),
+        scratch_shapes=[
+            pltpu.VMEM((rows, inputs), jnp.bfloat16),
+            pltpu.VMEM((inputs // 128, rows, 128), jnp.float32),
+        ],
+        cost_estimate=pl.CostEstimate(flops=8 * 10**9, bytes_accessed=4 << 20, transcendentals=0),
+        compiler_params=pltpu.CompilerParams(
+            dimension_semantics=("arbitrary",), vmem_limit_bytes=VMEM
+        ),
+        name="order_late",
+    )(late, perm)
+
+
+def correlate_kernel(scale, sizes, per_step, *refs):
     late_ref, early_ref, perm_ref = refs[:3]
-    out_ref, lhs_ref, z_ref = refs[-3:]
+    out_ref, lhs_ref, z_ref, ordered_ref = refs[-4:]
     step = pl.program_id(0)
-    width = BATCH * ROWS
     inputs = out_ref.shape[1]
-    pairs = BATCH // 2
-    units = st_count * pol_count
-
-    @pl.when(step % (GROUP // per_step) == 0)
+    span = PREP * PER_SLOT
+    count = 2 * sizes[1]
+    depth = PAIRS * count
+
+    @pl.when(step % (PREP // per_step) == 0)
     def _():
-        row = 0
-        for c in range(2):
-            for source in (early_ref, late_ref):
-                for tm in range(tm_count):
-                    for pair in range(pairs):
-                        at = c * width + pair * 128
-                        for st in range(st_count):
-                            for pol in range(pol_count):
-                                unit = st * pol_count + pol
-                                lhs_ref[row : row + GROUP, unit * 128 : (unit + 1) * 128] = source[
-                                    (st * tm_count + tm) * pol_count + pol, :, at : at + 128
-                                ]
-                        row += GROUP
-        for half in range(2):
-            turned = jnp.dot(
-                lhs_ref[...],
-                perm_ref[:, half * inputs : (half + 1) * inputs],
-                preferred_element_type=jnp.float32,
-            )
-            for j in range(inputs // 128):
-                z_ref[half * (inputs // 128) + j] = turned[:, j * 128 : (j + 1) * 128]
-
-    depth = 2 * tm_count * pairs
+        order_inputs(early_ref, perm_ref, lhs_ref, z_ref, sizes, span)
+        for slot in range(PREP):
+            for c in range(2):
+                ordered_ref[slot, c * depth : (c + 1) * depth, :] = slot_rows(z_ref, slot, c, span, count)
+
     mid = inputs // 2
     tall = lax.broadcasted_iota(jnp.int32, (mid, mid), 0)
     wide = lax.broadcasted_iota(jnp.int32, (mid, mid), 1)
     upper = tall <= wide
 
     def one(i, carry):
-        slot = lax.rem(step, GROUP // per_step) * per_step + i
-
-        def rows(half, c):
-            tiles = [
-                z_ref[
-                    half * (inputs // 128) + j,
-                    pl.ds(c * depth * GROUP + slot, depth, stride=GROUP),
-                    :,
-                ]
-                for j in range(inputs // 128)
-            ]
-            return jnp.concatenate(tiles, axis=1)
-
-        re0, im0, re1, im1 = rows(0, 0), rows(0, 1), rows(1, 0), rows(1, 1)
-        z = jnp.concatenate([re0, im0, re1, im1], axis=0)
-        turned = jnp.concatenate([-im0, re0, -im1, re1], axis=0).astype(jnp.bfloat16)
-        left = z.T.astype(jnp.bfloat16)
-        z = z.astype(jnp.bfloat16)
+        slot = lax.rem(step, PREP // per_step) * per_step + i
+        early = ordered_ref[slot]
+        late = late_ref[i]
+        z = jnp.concatenate([early, late], axis=0)
+        turned = jnp.concatenate(
+            [-early[depth:], early[:depth], -late[depth:], late[:depth]], axis=0
+        )
+        left = z.T
         dot = functools.partial(jnp.dot, preferred_element_type=jnp.float32)
         for h in range(2):
             here = slice(h * mid, (h + 1) * mid)
@@ -261,21 +299,19 @@
         out_ref[i, mid:, :mid] = dot(left[mid:], turned[:, :mid]) * scale
         return carry
 
-    lax.fori_loop(0, per_step, one, 0)
-
-
-def correlate(half, halves, share, inputs, scale, sizes, late, early, perm, before):
-    st_count, tm_count, pol_count = sizes
+    lax.fori_loop(0, per_step, one, 0, unroll=True)
+
+
+def correlate(start, part, share, inputs, scale, sizes, late, early, perm, before):
     per_step = 4
-    part = share // halves
-    steps = part // per_step
-    prep = GROUP // per_step
-    peers, _, wide = late.shape
-    first_prep = half * (part // GROUP)
-    first_step = half * steps
+    prep = PREP // per_step
+    peers = early.shape[0]
+    depth = late.shape[1]
+    span = PREP * PER_SLOT
+    rows = 2 * sizes[1] * span
     in_specs = [
-        pl.BlockSpec((peers, GROUP, wide), lambda i: (0, first_prep + i // prep, 0)),
-        pl.BlockSpec((peers, GROUP, wide), lambda i: (0, i // prep, 0)),
+        pl.BlockSpec((per_step, depth, inputs), lambda i: (start // per_step + i, 0, 0)),
+        pl.BlockSpec((peers, span, 128), lambda i: (0, i // prep, 0)),
         pl.BlockSpec(perm.shape, lambda i: (0, 0)),
     ]
     operands = [late, early, perm]
@@ -285,14 +321,15 @@
         operands.append(before)
         aliases = {3: 0}
     return pl.pallas_call(
-        functools.partial(correlate_kernel, scale, st_count, tm_count, pol_count, per_step),
+        functools.partial(correlate_kernel, scale, sizes, per_step),
         out_shape=jax.ShapeDtypeStruct((share, inputs, inputs), jnp.float32),
-        grid=(steps,),
+        grid=(part // per_step,),
         in_specs=in_specs,
-        out_specs=pl.BlockSpec((per_step, inputs, inputs), lambda i: (first_step + i, 0, 0)),
+        out_specs=pl.BlockSpec((per_step, inputs, inputs), lambda i: (start // per_step + i, 0, 0)),
         scratch_shapes=[
-            pltpu.VMEM((2 * 2 * tm_count * (BATCH // 2) * GROUP, perm.shape[0]), jnp.bfloat16),
-            pltpu.VMEM((2 * inputs // 128, 2 * 2 * tm_count * (BATCH // 2) * GROUP, 128), jnp.float32),
+            pltpu.VMEM((rows, inputs), jnp.bfloat16),
+            pltpu.VMEM((inputs // 128, rows, 128), jnp.float32),
+            pltpu.VMEM((PREP, depth, inputs), jnp.bfloat16),
         ],
         input_output_aliases=aliases,
         cost_estimate=pl.CostEstimate(
@@ -317,50 +354,53 @@
     pol = lax.axis_index("pol")
     place = jnp.stack([pol, lax.axis_index("tm")]).astype(jnp.int32)
 
-    tail = lax.dynamic_slice(
+    ending = lax.dynamic_slice(
         samples, (pol * ROWS, local_length - LEAD * NFFT), (ROWS, LEAD * NFFT)
     )
-    halo = lax.ppermute(tail, "tm", [(i, i + 1) for i in range(tm_count - 1)])
+    halo = lax.ppermute(ending, "tm", [(i, i + 1) for i in range(tm_count - 1)])
 
     e, f = channel_order % FRAME_A, channel_order // FRAME_A
     row = jnp.minimum(e, FRAME_A - e) * (2 * LOW) + jnp.where(e > HALF_E, LOW, 0) + f
-    pick = jnp.broadcast_to(row.astype(jnp.int32)[:, None], (CH, 128))
+    rows = (row * PER_SLOT).astype(jnp.int32)
     cosine, sine = np_twist()
-    consts = [
-        jnp.asarray(c) for c in (np_window(), np_first(), cosine, sine, np_second())
-    ] + [pick]
+    consts = [jnp.asarray(c) for c in (np_window(), np_first(), cosine, sine, np_second())]
 
     groups = ROWS // GROUP
     late = filterbank(
-        late_kernel, "filterbank_late", peers, share, 1, place, [samples],
-        [pl.BlockSpec((GROUP, local_length), lambda i, p: (p[0] * groups + i, 0))],
+        late_kernel, "filterbank_late", peers, [share], place, rows, [samples],
+        [pl.BlockSpec((GROUP, local_length), lambda i, p, r: (p[0] * groups + i, 0))],
         consts,
     )
     late = lax.all_to_all(late[0], AXES, split_axis=0, concat_axis=0, tiled=True)
+    tail = share * 3 // 8
+    parts = [share - tail, tail]
     early = filterbank(
-        early_kernel, "filterbank_early", peers, share, 2, place, [samples, halo, history],
+        early_kernel, "filterbank_early", peers, parts, place, rows, [samples, halo, history],
         [
-            pl.BlockSpec((GROUP, BATCH * NFFT), lambda i, p: (p[0] * groups + i, 0)),
-            pl.BlockSpec((GROUP, LEAD * NFFT), lambda i, p: (i, 0)),
-            pl.BlockSpec((GROUP, LEAD * NFFT), lambda i, p: (p[0] * groups + i, 0)),
+            pl.BlockSpec((GROUP, BATCH * NFFT), lambda i, p, r: (p[0] * groups + i, 0)),
+            pl.BlockSpec((GROUP, LEAD * NFFT), lambda i, p, r: (i, 0)),
+            pl.BlockSpec((GROUP, LEAD * NFFT), lambda i, p, r: (p[0] * groups + i, 0)),
         ],
         consts,
     )
-    early = [lax.all_to_all(x, AXES, split_axis=0, concat_axis=0, tiled=True) for x in early]
-
-    global_row = jnp.arange(inputs)
-    target = 2 * jnp.repeat(station_order, 2) + global_row % 2
+    line = jnp.arange(inputs)
+    target = 2 * jnp.repeat(station_order, 2) + line % 2
     keep = 1 - jnp.repeat(flagged, 2)
-    hot = (target[:, None] == jnp.arange(inputs)[None, :]) & (keep[None, :] == 1)
-    hot = hot.astype(jnp.bfloat16).reshape(st_count * pol_count, 1, ROWS, 1, inputs)
-    pair = jnp.eye(2, dtype=jnp.bfloat16).reshape(1, 2, 1, 2, 1)
-    perm = (hot * pair).reshape(2 * inputs, 2 * inputs)
+    perm = ((target[:, None] == line[None, :]) & (keep[None, :] == 1)).astype(jnp.bfloat16)
+
+    *early, perm = lax.optimization_barrier((*early, perm))
+    sizes = (st_count, tm_count, pol_count)
+    first = lax.all_to_all(early[0], AXES, split_axis=0, concat_axis=0, tiled=True)
+    late = order_late(share, sizes, late, perm)
+    rest, late = lax.optimization_barrier((early[1], late))
+    rest = lax.all_to_all(rest, AXES, split_axis=0, concat_axis=0, tiled=True)
 
     scale = 1.0 / (spec_local * tm_count)
-    sizes = (st_count, tm_count, pol_count)
     out = None
-    for half in range(2):
-        out = correlate(half, 2, share, inputs, scale, sizes, late, early[half], perm, out)
+    start = 0
+    for part, arrived in zip(parts, (first, rest)):
+        out = correlate(start, part, share, inputs, scale, sizes, late, arrived, perm, out)
+        start += part
     return out
 
 
@@ -507,8 +547,8 @@
         rows == ROWS * pol_count
         and frames == 2 * BATCH
         and tm_count == 4
-        and share % (2 * GROUP) == 0
-        and 256 % share == 0
+        and pol_count == 2
+        and share % (8 * PREP) == 0
         and samples.shape[0] % 256 == 0
     )
 

time: 170 us -> 152 us (0.89)
  waiting for transfers between devices: 25.1 us -> 57.1 us
  blocking collectives: 30 us -> 0 us
  Pallas kernels: 89.3 us -> 70.5 us
  starting transfers between devices: 13.3 us -> 18.3 us
  local copies, waits for them, and re-layouts: 8.46 us -> 3.49 us
    all_to_all x1 -> x0, blocking collectives: 30 us -> none  [fused_body(): lax.all_to_all(x, AXES, split_axis=0, concat_axis=0, tiled=True)]
    all_to_all x1 -> x2, waiting for transfers between devices: 0.59 us -> 24.6 us  [the longest x1 24.6 us: fused_body(): lax.all_to_all(early[0], AXES, split_axis=0, concat_axis=0, tiled=True)]
    pallas_call x4 -> x5, Pallas kernels: 89.3 us -> 70.5 us  [the longest x2 35.3 us: correlate(): pl.pallas_call(functools.partial(correlate_kernel, scale, sizes, per_step...]
    all_to_all x1, waiting for transfers between devices: 24.5 us -> 32.5 us  [fused_body(): lax.all_to_all(late[0], AXES, split_axis=0, concat_axis=0, tiled=True)]
    all_to_all x1 -> x2, starting transfers between devices: 3.62 us -> 8.42 us  [the longest x1 4.8 us: fused_body(): lax.all_to_all(early[0], AXES, split_axis=0, concat_axis=0, tiled=True)]
    unnamed x11 -> x10, local copies, waits for them, and re-layouts: 2.87 us -> 0.9 us
  transfers between devices with their start and end apart: 3 -> 4, of which waited for: 2 -> 2; matrix products, arithmetic and copies ran while one was open for 4% -> 2% of each run, Pallas kernels for 40% -> 37%
where the time goes in v2:
time: 152 us
  Pallas kernels  70.5 us (46%)
  waiting for transfers between devices  57.1 us (38%)
  starting transfers between devices  18.3 us (12%)
  local copies, waits for them, and re-layouts  3.49 us (2%)
  other arithmetic  2.23 us (1%)
    pallas_call x2, Pallas kernels, correlate(): pl.pallas_call(functools.partial(correlate_kernel, scale, sizes, per_step...  35.3 us
    all_to_all x1, waiting for transfers between devices, fused_body(): lax.all_to_all(late[0], AXES, split_axis=0, concat_axis=0, tiled=True)  32.5 us
    pallas_call x2, Pallas kernels, filterbank(): pl.pallas_call(kernel, out_shape=outs, grid_spec=pltpu.PrefetchScalarGrid...  27.9 us
    all_to_all x1, waiting for transfers between devices, fused_body(): lax.all_to_all(early[0], AXES, split_axis=0, concat_axis=0, tiled=True)  24.6 us
    pallas_call x1, Pallas kernels, order_late(): pl.pallas_call(functools.partial(order_kernel, sizes), out_shape=jax.Shap...  7.29 us
    all_to_all x1, starting transfers between devices, fused_body(): lax.all_to_all(late[0], AXES, split_axis=0, concat_axis=0, tiled=True)  5.88 us
    all_to_all x1, starting transfers between devices, fused_body(): lax.all_to_all(early[0], AXES, split_axis=0, concat_axis=0, tiled=True)  4.8 us
    ppermute x1, starting transfers between devices, fused_body(): halo = lax.ppermute(ending, 'tm', [(i, i + 1) for i in range(tm_count - 1)])  3.99 us
  transfers between devices with their start and end apart: 4, of which 2 were waited for; matrix products, arithmetic and copies ran while one was open for 2% of the time, Pallas kernels for 37%

profile of v2, /device:TPU:0, one launch (start us, length us, event | category | flops | bytes accessed | tf_op | source)
XLA Modules:
  0.0 151.7 jit_solution(9381055633434922855)
XLA Ops:
  0.0 2.1 %constant_dynamic-slice_fusion = bf16[64,24576]{1,0:T(8,128)(2,1)S(1)} fusion(bf16[128,65536]{1,0:T(8,128)(2,1)} %x_ref.3, s32[]{:T(128)S(6)} %select_n.32), kind=kLoop, calls=%fused_computation.25 | loop fusion | bytes 6291460 | tf_op jit(solution)/shard_map/dynamic_slice | solution.py:357
  2.1 4.0 %collective-permute-start = (bf16[64,24576]{1,0:T(8,128)(2,1)S(1)}, bf16[64,24576]{1,0:T(8,128)(2,1)}, u32[]{:S(2)}, u32[]{:S(2)}) collective-permute-start(bf16[64,24576]{1,0:T(8,128)(2,1)S(1)} %constant_dynamic-slice_fusion), channel_id=1, source_target_pairs={{0,2},{2,4},{4,6},{1,3},{3,5},{5,7},{8,10},{10,12},{12,14},{9,11},... | collective-permute-start | bytes 9437192 | tf_op jit(solution)/shard_map/ppermute | solution.py:360
  6.1 0.0 copy-done.2
  6.1 0.6 fusion.5.row_ref
  6.7 0.6 pad_add_fusion.place_ref
  7.3 13.3 %filterbank_late.1 = bf16[32,256,128]{2,1,0:T(8,128)(2,1)} custom-call(s32[2]{0:T(128)} %pad_add_fusion.place_ref, s32[2048]{0:T(1024)} %fusion.5.row_ref, bf16[128,65536]{1,0:T(8,128)(2,1)} %x_ref.3, f32[4,8192]{1,0:T(4,128)} %constant.76.clone.w_ref, bf16[512,512]{1,0:T(8,128)(2,1)} %constant.77.clone.c1_ref, f32[17,256]{1,0:T(8,128)} %constant.78.clone.cos_ref, ...), custom_call_target="tpu_custom_call" | custom-call | flops 12000000000 | bytes 16777216 | tf_op jit(solution)/shard_map/filterbank_late/pallas_call | solution.py:170
  20.6 5.9 %all-to-all-start = ((bf16[32,256,128]{2,1,0:T(8,128)(2,1)}), bf16[32,256,128]{2,1,0:T(8,128)(2,1)}, u32[]{:S(2)}, u32[]{:S(2)}) async-start(bf16[32,256,128]{2,1,0:T(8,128)(2,1)} %filterbank_late.1), calls=%async_computation | async-start | bytes 4194304 | tf_op jit(solution)/shard_map/all_to_all | solution.py:374
  26.5 0.0 copy-done.4
  26.5 0.1 broadcast_in_dim.17
  26.6 0.2 eq.34
  26.8 0.1 broadcast_in_dim.16
  26.9 0.1 mul.38
  27.0 1.0 fusion.1.perm_ref.refs_2_
  28.1 0.0 collective-permute-done.halo_ref
  28.1 14.6 %filterbank_early.1 = (bf16[32,160,128]{2,1,0:T(8,128)(2,1)}, bf16[32,96,128]{2,1,0:T(8,128)(2,1)}) custom-call(s32[2]{0:T(128)} %pad_add_fusion.place_ref, s32[2048]{0:T(1024)} %fusion.5.row_ref, bf16[128,65536]{1,0:T(8,128)(2,1)} %x_ref.3, bf16[64,24576]{1,0:T(8,128)(2,1)} %collective-permute-done.halo_ref, bf16[128,24576]{1,0:T(8,128)(2,1)} %history_ref.1, ...), custom_call_target="tpu_custom_call" | custom-call | flops 12000000000 | bytes 16777216 | tf_op jit(solution)/shard_map/filterbank_early/pallas_call | solution.py:170
  42.7 32.5 %all-to-all-done.late_ref = bf16[32,256,128]{2,1,0:T(8,128)(2,1)} async-done(((bf16[32,256,128]{2,1,0:T(8,128)(2,1)}), bf16[32,256,128]{2,1,0:T(8,128)(2,1)}, u32[]{:S(2)}, u32[]{:S(2)}) %all-to-all-start) | async-done | bytes 2097184 | tf_op jit(solution)/shard_map/all_to_all | solution.py:374
  75.2 4.8 %all-to-all-start.2 = ((bf16[32,160,128]{2,1,0:T(8,128)(2,1)}), bf16[32,160,128]{2,1,0:T(8,128)(2,1)S(1)}, u32[]{:S(2)}, u32[]{:S(2)}) async-start(bf16[32,160,128]{2,1,0:T(8,128)(2,1)} %get-tuple-element.18), calls=%async_computation.2 | async-start | bytes 2621440 | tf_op jit(solution)/shard_map/all_to_all | solution.py:393
  80.0 7.3 %order_late.1.refs_0_ = bf16[64,32,512]{2,1,0:T(8,128)(2,1)} custom-call(bf16[32,256,128]{2,1,0:T(8,128)(2,1)} %all-to-all-done.late_ref, bf16[512,512]{1,0:T(8,128)(2,1)} %fusion.1.perm_ref.refs_2_), custom_call_target="tpu_custom_call" | custom-call | flops 8000000000 | bytes 4194304 | tf_op jit(solution)/shard_map/order_late/pallas_call | solution.py:241
  87.3 24.6 %all-to-all-done.2.refs_1_ = bf16[32,160,128]{2,1,0:T(8,128)(2,1)S(1)} async-done(((bf16[32,160,128]{2,1,0:T(8,128)(2,1)}), bf16[32,160,128]{2,1,0:T(8,128)(2,1)S(1)}, u32[]{:S(2)}, u32[]{:S(2)}) %all-to-all-start.2) | async-done | bytes 1310752 | tf_op jit(solution)/shard_map/all_to_all | solution.py:393
  111.8 3.6 %all-to-all-start.1 = ((bf16[32,96,128]{2,1,0:T(8,128)(2,1)}), bf16[32,96,128]{2,1,0:T(8,128)(2,1)S(1)}, u32[]{:S(2)}, u32[]{:S(2)}) async-start(bf16[32,96,128]{2,1,0:T(8,128)(2,1)} %get-tuple-element.17), calls=%async_computation.1 | async-start | bytes 1572864 | tf_op jit(solution)/shard_map/all_to_all | solution.py:396
  115.5 21.4 %correlate.2.refs_3_ = f32[64,512,512]{2,1,0:T(8,128)} custom-call(bf16[64,32,512]{2,1,0:T(8,128)(2,1)} %order_late.1.refs_0_, bf16[32,160,128]{2,1,0:T(8,128)(2,1)} %copy-done, bf16[512,512]{1,0:T(8,128)(2,1)} %fusion.1.perm_ref.refs_2_), custom_call_target="tpu_custom_call" | custom-call | flops 4800000000 | bytes 41943040 | tf_op jit(solution)/shard_map/correlate/pallas_call | solution.py:323
  136.9 0.0 all-to-all-done.1.refs_1_
  136.9 0.9 copy-done.1
  137.8 13.9 %correlate.3 = f32[64,512,512]{2,1,0:T(8,128)} custom-call(bf16[64,32,512]{2,1,0:T(8,128)(2,1)} %order_late.1.refs_0_, bf16[32,96,128]{2,1,0:T(8,128)(2,1)} %copy-done.1, bf16[512,512]{1,0:T(8,128)(2,1)} %fusion.1.perm_ref.refs_2_, f32[64,512,512]{2,1,0:T(8,128)} %correlate.2.refs_3_), custom_call_target="tpu_custom_call", output_to_operand_aliasing={{}: (3, {})} | custom-call | flops 2880000000 | bytes 25165824 | tf_op jit(solution)/shard_map/correlate/pallas_call | solution.py:323
  (10 shorter events, 0.0 us)
Async XLA Ops:
  0.0 6.1 %copy-start.2 = (s32[2048]{0:T(1024)S(1)}, s32[2048]{0:T(1024)}, u32[]{:S(2)}) copy-start(s32[2048]{0:T(1024)} %param.13) | copy-start | bytes 24580
  2.1 25.9 %collective-permute-start = (bf16[64,24576]{1,0:T(8,128)(2,1)S(1)}, bf16[64,24576]{1,0:T(8,128)(2,1)}, u32[]{:S(2)}, u32[]{:S(2)}) collective-permute-start(bf16[64,24576]{1,0:T(8,128)(2,1)S(1)} %constant_dynamic-slice_fusion), channel_id=1, source_target_pairs={{0,2},{2,4},{4,6},{1,3},{3,5},{5,7},{8,10},{10,12},{12,14},{9,11},... | collective-permute-start | bytes 9437192 | tf_op jit(solution)/shard_map/ppermute | solution.py:360
  20.6 5.9 %copy-start.4 = (s32[256]{0:T(256)S(1)}, s32[256]{0:T(256)}, u32[]{:S(2)}) copy-start(s32[256]{0:T(256)} %param.14) | copy-start | bytes 3076
  20.6 6.2 %copy-start.3 = (s32[256]{0:T(256)S(1)}, s32[256]{0:T(256)}, u32[]{:S(2)}) copy-start(s32[256]{0:T(256)} %param.12) | copy-start | bytes 3076
  20.6 54.6 %all-to-all-start = ((bf16[32,256,128]{2,1,0:T(8,128)(2,1)}), bf16[32,256,128]{2,1,0:T(8,128)(2,1)}, u32[]{:S(2)}, u32[]{:S(2)}) async-start(bf16[32,256,128]{2,1,0:T(8,128)(2,1)} %filterbank_late.1), calls=%async_computation | async-start | bytes 4194304 | tf_op jit(solution)/shard_map/all_to_all | solution.py:374
  75.2 36.7 %all-to-all-start.2 = ((bf16[32,160,128]{2,1,0:T(8,128)(2,1)}), bf16[32,160,128]{2,1,0:T(8,128)(2,1)S(1)}, u32[]{:S(2)}, u32[]{:S(2)}) async-start(bf16[32,160,128]{2,1,0:T(8,128)(2,1)} %get-tuple-element.18), calls=%async_computation.2 | async-start | bytes 2621440 | tf_op jit(solution)/shard_map/all_to_all | solution.py:393
  111.8 3.6 %copy-start = (bf16[32,160,128]{2,1,0:T(8,128)(2,1)}, bf16[32,160,128]{2,1,0:T(8,128)(2,1)S(1)}, u32[]{:S(2)}) copy-start(bf16[32,160,128]{2,1,0:T(8,128)(2,1)S(1)} %all-to-all-done.2.refs_1_) | copy-start | bytes 3932164
  111.8 25.1 %all-to-all-start.1 = ((bf16[32,96,128]{2,1,0:T(8,128)(2,1)}), bf16[32,96,128]{2,1,0:T(8,128)(2,1)S(1)}, u32[]{:S(2)}, u32[]{:S(2)}) async-start(bf16[32,96,128]{2,1,0:T(8,128)(2,1)} %get-tuple-element.17), calls=%async_computation.1 | async-start | bytes 1572864 | tf_op jit(solution)/shard_map/all_to_all | solution.py:396
  136.9 0.9 copy-start.1

commit v3 on v2

--- a/solution.py
+++ b/solution.py
@@ -21,10 +21,13 @@
 ROWS = 64
 GROUP = 16
 PREP = 8
+BATCHED = 2
+UNROLLED = 3
 BATCH = 4
 PAIRS = BATCH // 2
 PER_SLOT = 2 * PAIRS
-VMEM = 56 << 20
+VMEM = 62 << 20
+BANK_VMEM = 56 << 20
 
 
 def np_window():
@@ -63,10 +66,10 @@
     return np.concatenate([top, bottom]).astype(jnp.bfloat16)
 
 
-def filterbank_body(taps_of, step, refs):
+def filterbank_body(sources, step, refs):
     row_ref, w_ref, c1_ref, cos_ref, sin_ref, w2_ref, outs, y_ref, t_ref, d_ref = refs
 
-    def filter_a(a, carry):
+    def filter_a(taps_of, a, carry):
         weights = [w_ref[k : k + 1, pl.ds(pl.multiple_of(a * FRAME_B, FRAME_B), FRAME_B)] for k in range(TAPS)]
         frames = [taps_of(i, a) for i in range(BATCH + LEAD)]
         for t in range(BATCH):
@@ -76,7 +79,18 @@
             y_ref[t, pl.ds(pl.multiple_of(a * GROUP, GROUP), GROUP), :] = total.astype(jnp.bfloat16)
         return carry
 
-    lax.fori_loop(0, FRAME_A, filter_a, 0, unroll=2)
+    if len(sources) == 1:
+        lax.fori_loop(0, FRAME_A, functools.partial(filter_a, sources[0]), 0, unroll=2)
+    else:
+        opening = row_ref[CH + 1] == 0
+
+        @pl.when(opening)
+        def _():
+            lax.fori_loop(0, FRAME_A, functools.partial(filter_a, sources[0]), 0, unroll=2)
+
+        @pl.when(jnp.logical_not(opening))
+        def _():
+            lax.fori_loop(0, FRAME_A, functools.partial(filter_a, sources[1]), 0, unroll=2)
 
     def first_t(t, carry):
         seg = jnp.dot(c1_ref[...], y_ref[t], preferred_element_type=jnp.float32)
@@ -133,7 +147,7 @@
         lax.fori_loop(0, outs[0].shape[0], gather, 0)
 
 
-def late_kernel(place_ref, row_ref, x_ref, w_ref, c1_ref, cos_ref, sin_ref, w2_ref, *rest):
+def late_kernel(row_ref, x_ref, w_ref, c1_ref, cos_ref, sin_ref, w2_ref, *rest):
     outs, (y_ref, t_ref, d_ref) = rest[:-3], rest[-3:]
     first = x_ref.shape[1] // NFFT - BATCH
 
@@ -142,39 +156,37 @@
         return x_ref[:, pl.ds(pl.multiple_of(at + a * FRAME_B, FRAME_B), FRAME_B)].astype(jnp.float32)
 
     refs = (row_ref, w_ref, c1_ref, cos_ref, sin_ref, w2_ref, outs, y_ref, t_ref, d_ref)
-    filterbank_body(taps_of, pl.program_id(0), refs)
+    filterbank_body([taps_of], pl.program_id(0), refs)
 
 
 def early_kernel(
-    place_ref, row_ref, x_ref, halo_ref, history_ref, w_ref, c1_ref, cos_ref, sin_ref, w2_ref, *rest
+    row_ref, x_ref, halo_ref, history_ref, w_ref, c1_ref, cos_ref, sin_ref, w2_ref, *rest
 ):
     outs, (y_ref, t_ref, d_ref) = rest[:-3], rest[-3:]
-    opening = place_ref[1] == 0
-
-    def taps_of(i, a):
-        if i >= LEAD:
-            at = pl.multiple_of((i - LEAD) * NFFT + a * FRAME_B, FRAME_B)
-            return x_ref[:, pl.ds(at, FRAME_B)].astype(jnp.float32)
-        at = pl.multiple_of(i * NFFT + a * FRAME_B, FRAME_B)
-        mine = halo_ref[:, pl.ds(at, FRAME_B)].astype(jnp.float32)
-        old = history_ref[:, pl.ds(at, FRAME_B)].astype(jnp.float32)
-        return jnp.where(opening, old, mine)
+
+    def taps_from(ahead_ref):
+        def taps_of(i, a):
+            source, at = (x_ref, i - LEAD) if i >= LEAD else (ahead_ref, i)
+            at = pl.multiple_of(at * NFFT + a * FRAME_B, FRAME_B)
+            return source[:, pl.ds(at, FRAME_B)].astype(jnp.float32)
+
+        return taps_of
 
     refs = (row_ref, w_ref, c1_ref, cos_ref, sin_ref, w2_ref, outs, y_ref, t_ref, d_ref)
-    filterbank_body(taps_of, pl.program_id(0), refs)
-
-
-def filterbank(kernel, name, peers, parts, place, rows, streams, stream_specs, consts):
-    whole = [pl.BlockSpec(c.shape, lambda i, p, r: (0, 0)) for c in consts]
+    filterbank_body([taps_from(history_ref), taps_from(halo_ref)], pl.program_id(0), refs)
+
+
+def filterbank(kernel, name, peers, parts, rows, streams, stream_specs, consts):
+    whole = [pl.BlockSpec(c.shape, lambda i, r: (0, 0)) for c in consts]
     outs = [jax.ShapeDtypeStruct((peers, part * PER_SLOT, 128), jnp.bfloat16) for part in parts]
     return pl.pallas_call(
         kernel,
         out_shape=outs,
         grid_spec=pltpu.PrefetchScalarGridSpec(
-            num_scalar_prefetch=2,
+            num_scalar_prefetch=1,
             grid=(ROWS // GROUP,),
             in_specs=stream_specs + whole,
-            out_specs=[pl.BlockSpec(out.shape, lambda i, p, r: (0, 0, 0)) for out in outs],
+            out_specs=[pl.BlockSpec(out.shape, lambda i, r: (0, 0, 0)) for out in outs],
             scratch_shapes=[
                 pltpu.VMEM((BATCH, FRAME_A * GROUP, FRAME_B), jnp.bfloat16),
                 pltpu.VMEM((HALF_E + 1, BATCH * ROWS, 2 * FRAME_B), jnp.bfloat16),
@@ -183,10 +195,10 @@
         ),
         cost_estimate=pl.CostEstimate(flops=12 * 10**9, bytes_accessed=16 << 20, transcendentals=0),
         compiler_params=pltpu.CompilerParams(
-            dimension_semantics=("arbitrary",), vmem_limit_bytes=VMEM
+            dimension_semantics=("arbitrary",), vmem_limit_bytes=BANK_VMEM
         ),
         name=name,
-    )(place, rows, *streams, *consts)
+    )(rows, *streams, *consts)
 
 
 def order_inputs(source, perm_ref, lhs_ref, z_ref, sizes, span):
@@ -232,21 +244,21 @@
             )
 
 
-def order_late(share, sizes, late, perm):
+def order_late(part, sizes, late, perm):
     peers = late.shape[0]
     inputs = perm.shape[1]
-    span = GROUP * PER_SLOT
+    span = PREP * PER_SLOT
     rows = 2 * sizes[1] * span
     depth = 2 * sizes[1] * PER_SLOT
     return pl.pallas_call(
         functools.partial(order_kernel, sizes),
-        out_shape=jax.ShapeDtypeStruct((share, depth, inputs), jnp.bfloat16),
-        grid=(share // GROUP,),
+        out_shape=jax.ShapeDtypeStruct((part, depth, inputs), jnp.bfloat16),
+        grid=(part // PREP,),
         in_specs=[
             pl.BlockSpec((peers, span, 128), lambda i: (0, i, 0)),
             pl.BlockSpec(perm.shape, lambda i: (0, 0)),
         ],
-        out_specs=pl.BlockSpec((GROUP, depth, inputs), lambda i: (i, 0, 0)),
+        out_specs=pl.BlockSpec((PREP, depth, inputs), lambda i: (i, 0, 0)),
         scratch_shapes=[
             pltpu.VMEM((rows, inputs), jnp.bfloat16),
             pltpu.VMEM((inputs // 128, rows, 128), jnp.float32),
@@ -259,77 +271,107 @@
     )(late, perm)
 
 
-def correlate_kernel(scale, sizes, per_step, *refs):
-    late_ref, early_ref, perm_ref = refs[:3]
-    out_ref, lhs_ref, z_ref, ordered_ref = refs[-4:]
-    step = pl.program_id(0)
-    inputs = out_ref.shape[1]
+def correlate_kernel(scale, sizes, start, *refs):
+    late_ref, arrived_ref, perm_ref = refs[:3]
+    out_ref, lhs_ref, z_ref, ordered_ref, buffer_ref, sems = refs[-6:]
+    inputs = perm_ref.shape[1]
     span = PREP * PER_SLOT
     count = 2 * sizes[1]
     depth = PAIRS * count
-
-    @pl.when(step % (PREP // per_step) == 0)
-    def _():
-        order_inputs(early_ref, perm_ref, lhs_ref, z_ref, sizes, span)
+    batches, batch = buffer_ref.shape[:2]
+    tile = 128
+    tall = lax.broadcasted_iota(jnp.int32, (tile, tile), 0)
+    wide = lax.broadcasted_iota(jnp.int32, (tile, tile), 1)
+    upper = tall <= wide
+
+    def leave(group, k):
+        first = start + group * PREP + k * batch
+        return pltpu.make_async_copy(
+            buffer_ref.at[k], out_ref.at[pl.ds(first, batch)], sems.at[k]
+        )
+
+    def products(z, turned, left, into):
+        for at in range(0, inputs, tile):
+            rows = slice(at, at + tile)
+            sides = jnp.concatenate([turned[:, : at + tile], z[:, at:]], axis=1)
+            both = jnp.dot(left[rows], sides, preferred_element_type=jnp.float32) * scale
+            if at > 0:
+                into[rows, :at] = both[:, :at]
+            into[rows, rows] = jnp.where(
+                upper, both[:, at + tile : at + 2 * tile], both[:, at : at + tile]
+            )
+            if at + tile < inputs:
+                into[rows, at + tile :] = both[:, at + 2 * tile :]
+
+    def order(group, parity):
+        source = arrived_ref.at[:, pl.ds(pl.multiple_of(group * span, span), span), :]
+        order_inputs(source, perm_ref, lhs_ref, z_ref, sizes, span)
         for slot in range(PREP):
             for c in range(2):
-                ordered_ref[slot, c * depth : (c + 1) * depth, :] = slot_rows(z_ref, slot, c, span, count)
-
-    mid = inputs // 2
-    tall = lax.broadcasted_iota(jnp.int32, (mid, mid), 0)
-    wide = lax.broadcasted_iota(jnp.int32, (mid, mid), 1)
-    upper = tall <= wide
-
-    def one(i, carry):
-        slot = lax.rem(step, PREP // per_step) * per_step + i
-        early = ordered_ref[slot]
-        late = late_ref[i]
-        z = jnp.concatenate([early, late], axis=0)
-        turned = jnp.concatenate(
-            [-early[depth:], early[:depth], -late[depth:], late[:depth]], axis=0
-        )
-        left = z.T
-        dot = functools.partial(jnp.dot, preferred_element_type=jnp.float32)
-        for h in range(2):
-            here = slice(h * mid, (h + 1) * mid)
-            re = dot(left[here], z[:, here])
-            im = dot(left[here], turned[:, here])
-            out_ref[i, here, here] = jnp.where(upper, re, im) * scale
-        out_ref[i, :mid, mid:] = dot(left[:mid], z[:, mid:]) * scale
-        out_ref[i, mid:, :mid] = dot(left[mid:], turned[:, :mid]) * scale
-        return carry
-
-    lax.fori_loop(0, per_step, one, 0, unroll=True)
-
-
-def correlate(start, part, share, inputs, scale, sizes, late, early, perm, before):
-    per_step = 4
-    prep = PREP // per_step
-    peers = early.shape[0]
+                ordered_ref[parity, slot, c * depth : (c + 1) * depth, :] = slot_rows(
+                    z_ref, slot, c, span, count
+                )
+
+    groups = late_ref.shape[0] // PREP
+
+    def work(group, parity, fresh, following):
+        for k in range(batches):
+            if not fresh:
+                leave(group - 1, k).wait()
+            if k == 1 and following is not None:
+                order(following, 1 - parity)
+            for i in range(batch):
+                slot = k * batch + i
+                z = jnp.concatenate([ordered_ref[parity, slot], late_ref[group * PREP + slot]], axis=0)
+                turned = []
+                for at in range(0, z.shape[0], 2 * depth):
+                    turned += [-z[at + depth : at + 2 * depth], z[at : at + depth]]
+                turned = jnp.concatenate(turned, axis=0)
+                products(z, turned, z.T, buffer_ref.at[k, i])
+            leave(group, k).start()
+
+    order(0, 0)
+    if groups <= UNROLLED:
+        for group in range(groups):
+            work(group, group % 2, group == 0, group + 1 if group + 1 < groups else None)
+    else:
+
+        def follow(group, carry):
+            work(group, lax.rem(group, 2), False, jnp.minimum(group + 1, groups - 1))
+            return carry
+
+        work(0, 0, True, 1)
+        lax.fori_loop(1, groups, follow, 0)
+    for k in range(batches):
+        leave(groups - 1, k).wait()
+
+
+def correlate(start, part, share, inputs, scale, sizes, late, arrived, perm, before):
     depth = late.shape[1]
-    span = PREP * PER_SLOT
-    rows = 2 * sizes[1] * span
+    rows = 2 * sizes[1] * PREP * PER_SLOT
+    operands = [late, arrived, perm]
     in_specs = [
-        pl.BlockSpec((per_step, depth, inputs), lambda i: (start // per_step + i, 0, 0)),
-        pl.BlockSpec((peers, span, 128), lambda i: (0, i // prep, 0)),
+        pl.BlockSpec((pl.Element(part), pl.Element(depth), pl.Element(inputs)), lambda i: (start, 0, 0)),
+        pl.BlockSpec(arrived.shape, lambda i: (0, 0, 0)),
         pl.BlockSpec(perm.shape, lambda i: (0, 0)),
     ]
-    operands = [late, early, perm]
     aliases = {}
     if before is not None:
         in_specs.append(pl.BlockSpec(memory_space=pl.ANY))
+        aliases = {len(operands): 0}
         operands.append(before)
-        aliases = {3: 0}
     return pl.pallas_call(
-        functools.partial(correlate_kernel, scale, sizes, per_step),
+        functools.partial(correlate_kernel, scale, sizes, start),
         out_shape=jax.ShapeDtypeStruct((share, inputs, inputs), jnp.float32),
-        grid=(part // per_step,),
+        grid=(1,),
         in_specs=in_specs,
-        out_specs=pl.BlockSpec((per_step, inputs, inputs), lambda i: (start // per_step + i, 0, 0)),
+        out_specs=pl.BlockSpec(memory_space=pl.ANY),
         scratch_shapes=[
             pltpu.VMEM((rows, inputs), jnp.bfloat16),
             pltpu.VMEM((inputs // 128, rows, 128), jnp.float32),
-            pltpu.VMEM((PREP, depth, inputs), jnp.bfloat16),
+            pltpu.VMEM((2, PREP, depth, inputs), jnp.bfloat16),
+            pltpu.VMEM((PREP // BATCHED, BATCHED, inputs, inputs), jnp.float32),
+            pltpu.SemaphoreType.DMA((PREP // BATCHED,)),
         ],
         input_output_aliases=aliases,
         cost_estimate=pl.CostEstimate(
@@ -352,7 +394,6 @@
     share = CH // peers
     inputs = row_count * st_count
     pol = lax.axis_index("pol")
-    place = jnp.stack([pol, lax.axis_index("tm")]).astype(jnp.int32)
 
     ending = lax.dynamic_slice(
         samples, (pol * ROWS, local_length - LEAD * NFFT), (ROWS, LEAD * NFFT)
@@ -361,25 +402,29 @@
 
     e, f = channel_order % FRAME_A, channel_order // FRAME_A
     row = jnp.minimum(e, FRAME_A - e) * (2 * LOW) + jnp.where(e > HALF_E, LOW, 0) + f
-    rows = (row * PER_SLOT).astype(jnp.int32)
+    rows = jnp.arange(CH + 2)
+    here = jnp.where(rows == CH, pol, lax.axis_index("tm"))
+    rows = jnp.where(rows < CH, jnp.pad(row * PER_SLOT, (0, 2)), here).astype(jnp.int32)
     cosine, sine = np_twist()
     consts = [jnp.asarray(c) for c in (np_window(), np_first(), cosine, sine, np_second())]
 
+    parts = [5 * (share // 8), 3 * (share // 8)]
     groups = ROWS // GROUP
     late = filterbank(
-        late_kernel, "filterbank_late", peers, [share], place, rows, [samples],
-        [pl.BlockSpec((GROUP, local_length), lambda i, p, r: (p[0] * groups + i, 0))],
+        late_kernel, "filterbank_late", peers, [share], rows, [samples],
+        [pl.BlockSpec((GROUP, local_length), lambda i, r: (r[CH] * groups + i, 0))],
         consts,
     )
-    late = lax.all_to_all(late[0], AXES, split_axis=0, concat_axis=0, tiled=True)
-    tail = share * 3 // 8
-    parts = [share - tail, tail]
+    exchange = functools.partial(lax.all_to_all, axis_name=AXES, split_axis=0, concat_axis=0, tiled=True)
+    late = exchange(late[0])
     early = filterbank(
-        early_kernel, "filterbank_early", peers, parts, place, rows, [samples, halo, history],
+        early_kernel, "filterbank_early", peers, parts, rows, [samples, halo, history],
         [
-            pl.BlockSpec((GROUP, BATCH * NFFT), lambda i, p, r: (p[0] * groups + i, 0)),
-            pl.BlockSpec((GROUP, LEAD * NFFT), lambda i, p, r: (i, 0)),
-            pl.BlockSpec((GROUP, LEAD * NFFT), lambda i, p, r: (p[0] * groups + i, 0)),
+            pl.BlockSpec((GROUP, BATCH * NFFT), lambda i, r: (r[CH] * groups + i, 0)),
+            pl.BlockSpec((GROUP, LEAD * NFFT), lambda i, r: (jnp.where(r[CH + 1] == 0, 0, i), 0)),
+            pl.BlockSpec(
+                (GROUP, LEAD * NFFT), lambda i, r: (jnp.where(r[CH + 1] == 0, r[CH] * groups + i, 0), 0)
+            ),
         ],
         consts,
     )
@@ -388,20 +433,17 @@
     keep = 1 - jnp.repeat(flagged, 2)
     perm = ((target[:, None] == line[None, :]) & (keep[None, :] == 1)).astype(jnp.bfloat16)
 
-    *early, perm = lax.optimization_barrier((*early, perm))
+    early, rest, perm = lax.optimization_barrier((*early, perm))
     sizes = (st_count, tm_count, pol_count)
-    first = lax.all_to_all(early[0], AXES, split_axis=0, concat_axis=0, tiled=True)
+    early = exchange(early)
     late = order_late(share, sizes, late, perm)
-    rest, late = lax.optimization_barrier((early[1], late))
-    rest = lax.all_to_all(rest, AXES, split_axis=0, concat_axis=0, tiled=True)
+    rest, late = lax.optimization_barrier((rest, late))
+    rest = exchange(rest)
 
     scale = 1.0 / (spec_local * tm_count)
-    out = None
-    start = 0
-    for part, arrived in zip(parts, (first, rest)):
-        out = correlate(start, part, share, inputs, scale, sizes, late, arrived, perm, out)
-        start += part
-    return out
+    common = (share, inputs, scale, sizes, late)
+    out = correlate(0, parts[0], *common, early, perm, None)
+    return correlate(parts[0], parts[1], *common, rest, perm, out)
 
 
 def shifted(array, axis, by):

time: 152 us -> 148 us (0.974)
  Pallas kernels: 70.5 us -> 64.7 us
  waiting for transfers between devices: 57.1 us -> 59.1 us
    pallas_call x2, Pallas kernels: 35.3 us -> 28.9 us  [correlate(): pl.pallas_call(functools.partial(correlate_kernel, scale, sizes, start),...]
    all_to_all x3, waiting for transfers between devices: 57.1 us -> 59.1 us  [the longest x1 33.4 us: fused_body(): late = exchange(late[0])]
    pallas_call x1, Pallas kernels: 7.29 us -> 8.85 us  [order_late(): pl.pallas_call(functools.partial(order_kernel, sizes), out_shape=jax.Shap...]
  transfers between devices with their start and end apart: 4 -> 4, of which waited for: 2 -> 3; matrix products, arithmetic and copies ran while one was open for 2% -> 1% of each run, Pallas kernels for 37% -> 36%
where the time goes in v3:
time: 148 us; the launch traced here: 147 us
  Pallas kernels  64.7 us (44%)
  waiting for transfers between devices  59.1 us (40%)
  starting transfers between devices  18.5 us (12%)
  local copies, waits for them, and re-layouts  2.6 us (2%)
  other arithmetic  1.66 us (1%)
    all_to_all x1, waiting for transfers between devices, fused_body(): late = exchange(late[0])  33.4 us
    pallas_call x2, Pallas kernels, correlate(): pl.pallas_call(functools.partial(correlate_kernel, scale, sizes, start),...  28.9 us
    pallas_call x2, Pallas kernels, filterbank(): pl.pallas_call(kernel, out_shape=outs, grid_spec=pltpu.PrefetchScalarGrid...  27 us
    all_to_all x1, waiting for transfers between devices, fused_body(): early = exchange(early)  23 us
    pallas_call x1, Pallas kernels, order_late(): pl.pallas_call(functools.partial(order_kernel, sizes), out_shape=jax.Shap...  8.85 us
    all_to_all x1, starting transfers between devices, fused_body(): late = exchange(late[0])  5.88 us
    all_to_all x1, starting transfers between devices, fused_body(): early = exchange(early)  4.71 us
    ppermute x1, starting transfers between devices, fused_body(): halo = lax.ppermute(ending, 'tm', [(i, i + 1) for i in range(tm_count - 1)])  3.99 us
  transfers between devices with their start and end apart: 4, of which 3 were waited for; matrix products, arithmetic and copies ran while one was open for 1% of the time, Pallas kernels for 36%

profile of v3, /device:TPU:0, one launch (start us, length us, event | category | flops | bytes accessed | tf_op | source)
XLA Modules:
  0.0 146.9 jit_solution(13290767408798693046)
XLA Ops:
  0.0 2.1 %constant_dynamic-slice_fusion = bf16[64,24576]{1,0:T(8,128)(2,1)S(1)} fusion(bf16[128,65536]{1,0:T(8,128)(2,1)} %x_ref.3, s32[]{:T(128)S(6)} %select_n.42), kind=kLoop, calls=%fused_computation.27 | loop fusion | bytes 6291460 | tf_op jit(solution)/shard_map/dynamic_slice | solution.py:398
  2.1 4.0 %collective-permute-start = (bf16[64,24576]{1,0:T(8,128)(2,1)S(1)}, bf16[64,24576]{1,0:T(8,128)(2,1)}, u32[]{:S(2)}, u32[]{:S(2)}) collective-permute-start(bf16[64,24576]{1,0:T(8,128)(2,1)S(1)} %constant_dynamic-slice_fusion), channel_id=1, source_target_pairs={{0,2},{2,4},{4,6},{1,3},{3,5},{5,7},{8,10},{10,12},{12,14},{9,11},... | collective-permute-start | bytes 9437192 | tf_op jit(solution)/shard_map/ppermute | solution.py:401
  6.1 0.0 copy-done.1
  6.1 0.6 select_select_fusion.row_ref
  6.7 13.3 %filterbank_late.1 = bf16[32,256,128]{2,1,0:T(8,128)(2,1)} custom-call(s32[2050]{0:T(1024)} %select_select_fusion.row_ref, bf16[128,65536]{1,0:T(8,128)(2,1)} %x_ref.3, f32[4,8192]{1,0:T(4,128)} %constant.78.clone.w_ref, bf16[512,512]{1,0:T(8,128)(2,1)} %constant.79.clone.c1_ref, f32[17,256]{1,0:T(8,128)} %constant.80.clone.cos_ref, ...), custom_call_target="tpu_custom_call" | custom-call | flops 12000000000 | bytes 16777216 | tf_op jit(solution)/shard_map/filterbank_late/pallas_call | solution.py:182
  20.0 5.9 %all-to-all-start = ((bf16[32,256,128]{2,1,0:T(8,128)(2,1)}), bf16[32,256,128]{2,1,0:T(8,128)(2,1)}, u32[]{:S(2)}, u32[]{:S(2)}) async-start(bf16[32,256,128]{2,1,0:T(8,128)(2,1)} %filterbank_late.1), calls=%async_computation | async-start | bytes 4194304 | tf_op jit(solution)/shard_map/all_to_all | solution.py:419
  25.9 0.0 copy-done.3
  25.9 0.1 broadcast_in_dim.27
  26.0 0.2 eq.38
  26.2 0.0 copy-done.2
  26.2 0.1 broadcast_in_dim.26
  26.3 0.1 mul.38
  26.5 1.0 fusion.1.perm_ref.refs_2_
  27.5 0.0 collective-permute-done.halo_ref
  27.5 13.7 %filterbank_early.1 = (bf16[32,160,128]{2,1,0:T(8,128)(2,1)}, bf16[32,96,128]{2,1,0:T(8,128)(2,1)}) custom-call(s32[2050]{0:T(1024)} %select_select_fusion.row_ref, bf16[128,65536]{1,0:T(8,128)(2,1)} %x_ref.3, bf16[64,24576]{1,0:T(8,128)(2,1)} %collective-permute-done.halo_ref, bf16[128,24576]{1,0:T(8,128)(2,1)} %history_ref.1, ...), custom_call_target="tpu_custom_call" | custom-call | flops 12000000000 | bytes 16777216 | tf_op jit(solution)/shard_map/filterbank_early/pallas_call | solution.py:182
  41.2 33.4 %all-to-all-done.late_ref = bf16[32,256,128]{2,1,0:T(8,128)(2,1)} async-done(((bf16[32,256,128]{2,1,0:T(8,128)(2,1)}), bf16[32,256,128]{2,1,0:T(8,128)(2,1)}, u32[]{:S(2)}, u32[]{:S(2)}) %all-to-all-start) | async-done | bytes 2097184 | tf_op jit(solution)/shard_map/all_to_all | solution.py:419
  74.6 4.7 %all-to-all-start.2 = ((bf16[32,160,128]{2,1,0:T(8,128)(2,1)}), bf16[32,160,128]{2,1,0:T(8,128)(2,1)S(1)}, u32[]{:S(2)}, u32[]{:S(2)}) async-start(bf16[32,160,128]{2,1,0:T(8,128)(2,1)} %get-tuple-element.18), calls=%async_computation.2 | async-start | bytes 2621440 | tf_op jit(solution)/shard_map/all_to_all | solution.py:438
  79.3 8.8 %order_late.1.refs_0_ = bf16[64,32,512]{2,1,0:T(8,128)(2,1)} custom-call(bf16[32,256,128]{2,1,0:T(8,128)(2,1)} %all-to-all-done.late_ref, bf16[512,512]{1,0:T(8,128)(2,1)} %fusion.1.perm_ref.refs_2_), custom_call_target="tpu_custom_call" | custom-call | flops 8000000000 | bytes 4194304 | tf_op jit(solution)/shard_map/order_late/pallas_call | solution.py:253
  88.2 23.0 %all-to-all-done.2.refs_1_ = bf16[32,160,128]{2,1,0:T(8,128)(2,1)S(1)} async-done(((bf16[32,160,128]{2,1,0:T(8,128)(2,1)}), bf16[32,160,128]{2,1,0:T(8,128)(2,1)S(1)}, u32[]{:S(2)}, u32[]{:S(2)}) %all-to-all-start.2) | async-done | bytes 1310752 | tf_op jit(solution)/shard_map/all_to_all | solution.py:438
  111.2 3.9 %all-to-all-start.1 = ((bf16[32,96,128]{2,1,0:T(8,128)(2,1)}), bf16[32,96,128]{2,1,0:T(8,128)(2,1)}, u32[]{:S(2)}, u32[]{:S(2)}) async-start(bf16[32,96,128]{2,1,0:T(8,128)(2,1)} %get-tuple-element.17), calls=%async_computation.1 | async-start | bytes 1572864 | tf_op jit(solution)/shard_map/all_to_all | solution.py:441
  115.1 0.0 copy-done
  115.1 17.7 %correlate.2.refs_3_ = f32[64,512,512]{2,1,0:T(8,128)} custom-call(bf16[64,32,512]{2,1,0:T(8,128)(2,1)} %order_late.1.refs_0_, bf16[32,160,128]{2,1,0:T(8,128)(2,1)} %copy-done, bf16[512,512]{1,0:T(8,128)(2,1)} %fusion.1.perm_ref.refs_2_), custom_call_target="tpu_custom_call" | custom-call | flops 4800000000 | bytes 41943040 | tf_op jit(solution)/shard_map/correlate/pallas_call | solution.py:363
  132.8 2.7 %all-to-all-done.1.refs_1_ = bf16[32,96,128]{2,1,0:T(8,128)(2,1)} async-done(((bf16[32,96,128]{2,1,0:T(8,128)(2,1)}), bf16[32,96,128]{2,1,0:T(8,128)(2,1)}, u32[]{:S(2)}, u32[]{:S(2)}) %all-to-all-start.1) | async-done | bytes 786464 | tf_op jit(solution)/shard_map/all_to_all | solution.py:441
  135.5 11.1 %correlate.3 = f32[64,512,512]{2,1,0:T(8,128)} custom-call(bf16[64,32,512]{2,1,0:T(8,128)(2,1)} %order_late.1.refs_0_, bf16[32,96,128]{2,1,0:T(8,128)(2,1)} %all-to-all-done.1.refs_1_, bf16[512,512]{1,0:T(8,128)(2,1)} %fusion.1.perm_ref.refs_2_, f32[64,512,512]{2,1,0:T(8,128)} %correlate.2.refs_3_), custom_call_target="tpu_custom_call", output_to_operand_aliasing={{}: (3, {})} | custom-call | flops 2880000000 | bytes 25165824 | tf_op jit(solution)/shard_map/correlate/pallas_call | solution.py:363
  (8 shorter events, 0.0 us)
Async XLA Ops:
  0.0 6.1 %copy-start.1 = (s32[2048]{0:T(1024)S(1)}, s32[2048]{0:T(1024)}, u32[]{:S(2)}) copy-start(s32[2048]{0:T(1024)} %param.13) | copy-start | bytes 24580
  2.1 25.4 %collective-permute-start = (bf16[64,24576]{1,0:T(8,128)(2,1)S(1)}, bf16[64,24576]{1,0:T(8,128)(2,1)}, u32[]{:S(2)}, u32[]{:S(2)}) collective-permute-start(bf16[64,24576]{1,0:T(8,128)(2,1)S(1)} %constant_dynamic-slice_fusion), channel_id=1, source_target_pairs={{0,2},{2,4},{4,6},{1,3},{3,5},{5,7},{8,10},{10,12},{12,14},{9,11},... | collective-permute-start | bytes 9437192 | tf_op jit(solution)/shard_map/ppermute | solution.py:401
  20.0 5.9 %copy-start.3 = (s32[256]{0:T(256)S(1)}, s32[256]{0:T(256)}, u32[]{:S(2)}) copy-start(s32[256]{0:T(256)} %param.14) | copy-start | bytes 3076
  20.0 6.2 %copy-start.2 = (s32[256]{0:T(256)S(1)}, s32[256]{0:T(256)}, u32[]{:S(2)}) copy-start(s32[256]{0:T(256)} %param.12) | copy-start | bytes 3076
  20.0 54.6 %all-to-all-start = ((bf16[32,256,128]{2,1,0:T(8,128)(2,1)}), bf16[32,256,128]{2,1,0:T(8,128)(2,1)}, u32[]{:S(2)}, u32[]{:S(2)}) async-start(bf16[32,256,128]{2,1,0:T(8,128)(2,1)} %filterbank_late.1), calls=%async_computation | async-start | bytes 4194304 | tf_op jit(solution)/shard_map/all_to_all | solution.py:419
  74.6 36.6 %all-to-all-start.2 = ((bf16[32,160,128]{2,1,0:T(8,128)(2,1)}), bf16[32,160,128]{2,1,0:T(8,128)(2,1)S(1)}, u32[]{:S(2)}, u32[]{:S(2)}) async-start(bf16[32,160,128]{2,1,0:T(8,128)(2,1)} %get-tuple-element.18), calls=%async_computation.2 | async-start | bytes 2621440 | tf_op jit(solution)/shard_map/all_to_all | solution.py:438
  111.2 3.9 %copy-start = (bf16[32,160,128]{2,1,0:T(8,128)(2,1)}, bf16[32,160,128]{2,1,0:T(8,128)(2,1)S(1)}, u32[]{:S(2)}) copy-start(bf16[32,160,128]{2,1,0:T(8,128)(2,1)S(1)} %all-to-all-done.2.refs_1_) | copy-start | bytes 3932164
  111.2 24.4 %all-to-all-start.1 = ((bf16[32,96,128]{2,1,0:T(8,128)(2,1)}), bf16[32,96,128]{2,1,0:T(8,128)(2,1)}, u32[]{:S(2)}, u32[]{:S(2)}) async-start(bf16[32,96,128]{2,1,0:T(8,128)(2,1)} %get-tuple-element.17), calls=%async_computation.1 | async-start | bytes 1572864 | tf_op jit(solution)/shard_map/all_to_all | solution.py:441

commit v4 on v3

--- a/solution.py
+++ b/solution.py
@@ -67,7 +67,7 @@
 
 
 def filterbank_body(sources, step, refs):
-    row_ref, w_ref, c1_ref, cos_ref, sin_ref, w2_ref, outs, y_ref, t_ref, d_ref = refs
+    row_ref, w_ref, c1_ref, cos_ref, sin_ref, w2_ref, results, y_ref, t_ref, d_ref, sems, *outs = refs
 
     def filter_a(taps_of, a, carry):
         weights = [w_ref[k : k + 1, pl.ds(pl.multiple_of(a * FRAME_B, FRAME_B), FRAME_B)] for k in range(TAPS)]
@@ -144,25 +144,37 @@
                     out_ref[peer, at : at + 4 * PER_SLOT, :] = jnp.concatenate(halves).astype(jnp.bfloat16)
             return carry
 
-        lax.fori_loop(0, outs[0].shape[0], gather, 0)
+        quarter = outs[0].shape[0] // 4
+        copies = []
+        for q in range(4):
+            lax.fori_loop(q * quarter, (q + 1) * quarter, gather, 0)
+            for n, (out_ref, result_ref) in enumerate(zip(outs, results)):
+                peers = pl.ds(q * quarter, quarter)
+                copies.append(
+                    pltpu.make_async_copy(out_ref.at[peers], result_ref.at[peers], sems.at[n, q])
+                )
+                copies[-1].start()
+        for copy in copies:
+            copy.wait()
 
 
 def late_kernel(row_ref, x_ref, w_ref, c1_ref, cos_ref, sin_ref, w2_ref, *rest):
-    outs, (y_ref, t_ref, d_ref) = rest[:-3], rest[-3:]
-    first = x_ref.shape[1] // NFFT - BATCH
+    count = (len(rest) - 4) // 2
+    results, scratch = rest[:count], rest[count:]
 
     def taps_of(i, a):
-        at = (first - LEAD + i) * NFFT
-        return x_ref[:, pl.ds(pl.multiple_of(at + a * FRAME_B, FRAME_B), FRAME_B)].astype(jnp.float32)
-
-    refs = (row_ref, w_ref, c1_ref, cos_ref, sin_ref, w2_ref, outs, y_ref, t_ref, d_ref)
+        at = pl.multiple_of(i * NFFT + a * FRAME_B, FRAME_B)
+        return x_ref[:, pl.ds(at, FRAME_B)].astype(jnp.float32)
+
+    refs = (row_ref, w_ref, c1_ref, cos_ref, sin_ref, w2_ref, results, *scratch)
     filterbank_body([taps_of], pl.program_id(0), refs)
 
 
 def early_kernel(
     row_ref, x_ref, halo_ref, history_ref, w_ref, c1_ref, cos_ref, sin_ref, w2_ref, *rest
 ):
-    outs, (y_ref, t_ref, d_ref) = rest[:-3], rest[-3:]
+    count = (len(rest) - 4) // 2
+    results, scratch = rest[:count], rest[count:]
 
     def taps_from(ahead_ref):
         def taps_of(i, a):
@@ -172,7 +184,7 @@
 
         return taps_of
 
-    refs = (row_ref, w_ref, c1_ref, cos_ref, sin_ref, w2_ref, outs, y_ref, t_ref, d_ref)
+    refs = (row_ref, w_ref, c1_ref, cos_ref, sin_ref, w2_ref, results, *scratch)
     filterbank_body([taps_from(history_ref), taps_from(halo_ref)], pl.program_id(0), refs)
 
 
@@ -186,11 +198,13 @@
             num_scalar_prefetch=1,
             grid=(ROWS // GROUP,),
             in_specs=stream_specs + whole,
-            out_specs=[pl.BlockSpec(out.shape, lambda i, r: (0, 0, 0)) for out in outs],
+            out_specs=[pl.BlockSpec(memory_space=pl.ANY)] * len(outs),
             scratch_shapes=[
                 pltpu.VMEM((BATCH, FRAME_A * GROUP, FRAME_B), jnp.bfloat16),
                 pltpu.VMEM((HALF_E + 1, BATCH * ROWS, 2 * FRAME_B), jnp.bfloat16),
                 pltpu.VMEM(((HALF_E + 1) * 2 * LOW * PER_SLOT + 2 * PER_SLOT, 128), jnp.float32),
+                pltpu.SemaphoreType.DMA((len(outs), 4)),
+                *[pltpu.VMEM(out.shape, out.dtype) for out in outs],
             ],
         ),
         cost_estimate=pl.CostEstimate(flops=12 * 10**9, bytes_accessed=16 << 20, transcendentals=0),
@@ -215,7 +229,7 @@
                 )
     turned = jnp.dot(lhs_ref[...], perm_ref[...], preferred_element_type=jnp.float32)
     for j in range(z_ref.shape[0]):
-        z_ref[j] = turned[:, j * 128 : (j + 1) * 128]
+        z_ref[j, : turned.shape[0]] = turned[:, j * 128 : (j + 1) * 128]
 
 
 def slot_rows(z_ref, slot, c, span, count):
@@ -261,7 +275,7 @@
         out_specs=pl.BlockSpec((PREP, depth, inputs), lambda i: (i, 0, 0)),
         scratch_shapes=[
             pltpu.VMEM((rows, inputs), jnp.bfloat16),
-            pltpu.VMEM((inputs // 128, rows, 128), jnp.float32),
+            pltpu.VMEM((inputs // 128, rows + PREP * PER_SLOT, 128), jnp.float32),
         ],
         cost_estimate=pl.CostEstimate(flops=8 * 10**9, bytes_accessed=4 << 20, transcendentals=0),
         compiler_params=pltpu.CompilerParams(
@@ -368,7 +382,7 @@
         out_specs=pl.BlockSpec(memory_space=pl.ANY),
         scratch_shapes=[
             pltpu.VMEM((rows, inputs), jnp.bfloat16),
-            pltpu.VMEM((inputs // 128, rows, 128), jnp.float32),
+            pltpu.VMEM((inputs // 128, rows + PREP * PER_SLOT, 128), jnp.float32),
             pltpu.VMEM((2, PREP, depth, inputs), jnp.bfloat16),
             pltpu.VMEM((PREP // BATCHED, BATCHED, inputs, inputs), jnp.float32),
             pltpu.SemaphoreType.DMA((PREP // BATCHED,)),
@@ -412,7 +426,12 @@
     groups = ROWS // GROUP
     late = filterbank(
         late_kernel, "filterbank_late", peers, [share], rows, [samples],
-        [pl.BlockSpec((GROUP, local_length), lambda i, r: (r[CH] * groups + i, 0))],
+        [
+            pl.BlockSpec(
+                (pl.Element(GROUP), pl.Element((BATCH + LEAD) * NFFT)),
+                lambda i, r: ((r[CH] * groups + i) * GROUP, local_length - (BATCH + LEAD) * NFFT),
+            )
+        ],
         consts,
     )
     exchange = functools.partial(lax.all_to_all, axis_name=AXES, split_axis=0, concat_axis=0, tiled=True)

time: 148 us -> 147 us (level)
  no operation moved by 1% of the time
where the time goes in v4:
time: 147 us; the launch traced here: 146 us
  Pallas kernels  63.6 us (43%)
  waiting for transfers between devices  59.6 us (41%)
  starting transfers between devices  18.6 us (13%)
  local copies, waits for them, and re-layouts  2.61 us (2%)
  other arithmetic  1.66 us (1%)
    all_to_all x1, waiting for transfers between devices, fused_body(): late = exchange(late[0])  33.9 us
    pallas_call x2, Pallas kernels, correlate(): pl.pallas_call(functools.partial(correlate_kernel, scale, sizes, start),...  28.9 us
    pallas_call x2, Pallas kernels, filterbank(): pl.pallas_call(kernel, out_shape=outs, grid_spec=pltpu.PrefetchScalarGrid...  25.9 us
    all_to_all x1, waiting for transfers between devices, fused_body(): early = exchange(early)  23 us
    pallas_call x1, Pallas kernels, order_late(): pl.pallas_call(functools.partial(order_kernel, sizes), out_shape=jax.Shap...  8.85 us
    all_to_all x1, starting transfers between devices, fused_body(): late = exchange(late[0])  5.88 us
    all_to_all x1, starting transfers between devices, fused_body(): early = exchange(early)  4.8 us
    ppermute x1, starting transfers between devices, fused_body(): halo = lax.ppermute(ending, 'tm', [(i, i + 1) for i in range(tm_count - 1)])  3.99 us
  transfers between devices with their start and end apart: 4, of which 3 were waited for; matrix products, arithmetic and copies ran while one was open for 1% of the time, Pallas kernels for 36%

profile of v4, /device:TPU:0, one launch (start us, length us, event | category | flops | bytes accessed | tf_op | source)
XLA Modules:
  0.0 146.4 jit_solution(4573062633755530801)
XLA Ops:
  0.0 2.1 %constant_dynamic-slice_fusion = bf16[64,24576]{1,0:T(8,128)(2,1)S(1)} fusion(bf16[128,65536]{1,0:T(8,128)(2,1)} %x_ref.3, s32[]{:T(128)S(6)} %select_n.42), kind=kLoop, calls=%fused_computation.27 | loop fusion | bytes 6291460 | tf_op jit(solution)/shard_map/dynamic_slice | solution.py:412
  2.1 4.0 %collective-permute-start = (bf16[64,24576]{1,0:T(8,128)(2,1)S(1)}, bf16[64,24576]{1,0:T(8,128)(2,1)}, u32[]{:S(2)}, u32[]{:S(2)}) collective-permute-start(bf16[64,24576]{1,0:T(8,128)(2,1)S(1)} %constant_dynamic-slice_fusion), channel_id=1, source_target_pairs={{0,2},{2,4},{4,6},{1,3},{3,5},{5,7},{8,10},{10,12},{12,14},{9,11},... | collective-permute-start | bytes 9437192 | tf_op jit(solution)/shard_map/ppermute | solution.py:415
  6.1 0.0 copy-done.1
  6.1 0.6 select_select_fusion.row_ref
  6.7 12.7 %filterbank_late.1 = bf16[32,256,128]{2,1,0:T(8,128)(2,1)} custom-call(s32[2050]{0:T(1024)} %select_select_fusion.row_ref, bf16[128,65536]{1,0:T(8,128)(2,1)} %x_ref.3, f32[4,8192]{1,0:T(4,128)} %constant.78.clone.w_ref, bf16[512,512]{1,0:T(8,128)(2,1)} %constant.79.clone.c1_ref, f32[17,256]{1,0:T(8,128)} %constant.80.clone.cos_ref, ...), custom_call_target="tpu_custom_call" | custom-call | flops 12000000000 | bytes 16777216 | tf_op jit(solution)/shard_map/filterbank_late/pallas_call | solution.py:194
  19.5 0.0 copy-start.3
  19.5 0.0 copy-start.2
  19.5 5.9 %all-to-all-start = ((bf16[32,256,128]{2,1,0:T(8,128)(2,1)}), bf16[32,256,128]{2,1,0:T(8,128)(2,1)}, u32[]{:S(2)}, u32[]{:S(2)}) async-start(bf16[32,256,128]{2,1,0:T(8,128)(2,1)} %filterbank_late.1), calls=%async_computation | async-start | bytes 4194304 | tf_op jit(solution)/shard_map/all_to_all | solution.py:438
  25.4 0.0 copy-done.3
  25.4 0.1 broadcast_in_dim.27
  25.5 0.2 eq.38
  25.7 0.1 broadcast_in_dim.26
  25.8 0.1 mul.38
  25.9 1.0 fusion.1.perm_ref.refs_2_
  27.0 0.0 collective-permute-done.halo_ref
  27.0 13.2 %filterbank_early.1 = (bf16[32,160,128]{2,1,0:T(8,128)(2,1)}, bf16[32,96,128]{2,1,0:T(8,128)(2,1)}) custom-call(s32[2050]{0:T(1024)} %select_select_fusion.row_ref, bf16[128,65536]{1,0:T(8,128)(2,1)} %x_ref.3, bf16[64,24576]{1,0:T(8,128)(2,1)} %collective-permute-done.halo_ref, bf16[128,24576]{1,0:T(8,128)(2,1)} %history_ref.1, ...), custom_call_target="tpu_custom_call" | custom-call | flops 12000000000 | bytes 16777216 | tf_op jit(solution)/shard_map/filterbank_early/pallas_call | solution.py:194
  40.2 33.9 %all-to-all-done.late_ref = bf16[32,256,128]{2,1,0:T(8,128)(2,1)} async-done(((bf16[32,256,128]{2,1,0:T(8,128)(2,1)}), bf16[32,256,128]{2,1,0:T(8,128)(2,1)}, u32[]{:S(2)}, u32[]{:S(2)}) %all-to-all-start) | async-done | bytes 2097184 | tf_op jit(solution)/shard_map/all_to_all | solution.py:438
  74.1 4.8 %all-to-all-start.2 = ((bf16[32,160,128]{2,1,0:T(8,128)(2,1)}), bf16[32,160,128]{2,1,0:T(8,128)(2,1)S(1)}, u32[]{:S(2)}, u32[]{:S(2)}) async-start(bf16[32,160,128]{2,1,0:T(8,128)(2,1)} %get-tuple-element.18), calls=%async_computation.2 | async-start | bytes 2621440 | tf_op jit(solution)/shard_map/all_to_all | solution.py:457
  78.9 8.8 %order_late.1.refs_0_ = bf16[64,32,512]{2,1,0:T(8,128)(2,1)} custom-call(bf16[32,256,128]{2,1,0:T(8,128)(2,1)} %all-to-all-done.late_ref, bf16[512,512]{1,0:T(8,128)(2,1)} %fusion.1.perm_ref.refs_2_), custom_call_target="tpu_custom_call" | custom-call | flops 8000000000 | bytes 4194304 | tf_op jit(solution)/shard_map/order_late/pallas_call | solution.py:267
  87.7 23.0 %all-to-all-done.2.refs_1_ = bf16[32,160,128]{2,1,0:T(8,128)(2,1)S(1)} async-done(((bf16[32,160,128]{2,1,0:T(8,128)(2,1)}), bf16[32,160,128]{2,1,0:T(8,128)(2,1)S(1)}, u32[]{:S(2)}, u32[]{:S(2)}) %all-to-all-start.2) | async-done | bytes 1310752 | tf_op jit(solution)/shard_map/all_to_all | solution.py:457
  110.8 3.9 %all-to-all-start.1 = ((bf16[32,96,128]{2,1,0:T(8,128)(2,1)}), bf16[32,96,128]{2,1,0:T(8,128)(2,1)}, u32[]{:S(2)}, u32[]{:S(2)}) async-start(bf16[32,96,128]{2,1,0:T(8,128)(2,1)} %get-tuple-element.17), calls=%async_computation.1 | async-start | bytes 1572864 | tf_op jit(solution)/shard_map/all_to_all | solution.py:460
  114.7 17.7 %correlate.2.refs_3_ = f32[64,512,512]{2,1,0:T(8,128)} custom-call(bf16[64,32,512]{2,1,0:T(8,128)(2,1)} %order_late.1.refs_0_, bf16[32,160,128]{2,1,0:T(8,128)(2,1)} %copy-done, bf16[512,512]{1,0:T(8,128)(2,1)} %fusion.1.perm_ref.refs_2_), custom_call_target="tpu_custom_call" | custom-call | flops 4800000000 | bytes 41943040 | tf_op jit(solution)/shard_map/correlate/pallas_call | solution.py:377
  132.4 2.7 %all-to-all-done.1.refs_1_ = bf16[32,96,128]{2,1,0:T(8,128)(2,1)} async-done(((bf16[32,96,128]{2,1,0:T(8,128)(2,1)}), bf16[32,96,128]{2,1,0:T(8,128)(2,1)}, u32[]{:S(2)}, u32[]{:S(2)}) %all-to-all-start.1) | async-done | bytes 786464 | tf_op jit(solution)/shard_map/all_to_all | solution.py:460
  135.1 11.2 %correlate.3 = f32[64,512,512]{2,1,0:T(8,128)} custom-call(bf16[64,32,512]{2,1,0:T(8,128)(2,1)} %order_late.1.refs_0_, bf16[32,96,128]{2,1,0:T(8,128)(2,1)} %all-to-all-done.1.refs_1_, bf16[512,512]{1,0:T(8,128)(2,1)} %fusion.1.perm_ref.refs_2_, f32[64,512,512]{2,1,0:T(8,128)} %correlate.2.refs_3_), custom_call_target="tpu_custom_call", output_to_operand_aliasing={{}: (3, {})} | custom-call | flops 2880000000 | bytes 25165824 | tf_op jit(solution)/shard_map/correlate/pallas_call | solution.py:377
  (8 shorter events, 0.0 us)
Async XLA Ops:
  0.0 6.1 %copy-start.1 = (s32[2048]{0:T(1024)S(1)}, s32[2048]{0:T(1024)}, u32[]{:S(2)}) copy-start(s32[2048]{0:T(1024)} %param.13) | copy-start | bytes 24580
  2.1 24.8 %collective-permute-start = (bf16[64,24576]{1,0:T(8,128)(2,1)S(1)}, bf16[64,24576]{1,0:T(8,128)(2,1)}, u32[]{:S(2)}, u32[]{:S(2)}) collective-permute-start(bf16[64,24576]{1,0:T(8,128)(2,1)S(1)} %constant_dynamic-slice_fusion), channel_id=1, source_target_pairs={{0,2},{2,4},{4,6},{1,3},{3,5},{5,7},{8,10},{10,12},{12,14},{9,11},... | collective-permute-start | bytes 9437192 | tf_op jit(solution)/shard_map/ppermute | solution.py:415
  19.5 5.9 %copy-start.3 = (s32[256]{0:T(256)S(1)}, s32[256]{0:T(256)}, u32[]{:S(2)}) copy-start(s32[256]{0:T(256)} %param.14) | copy-start | bytes 3076
  19.5 6.2 %copy-start.2 = (s32[256]{0:T(256)S(1)}, s32[256]{0:T(256)}, u32[]{:S(2)}) copy-start(s32[256]{0:T(256)} %param.12) | copy-start | bytes 3076
  19.5 54.6 %all-to-all-start = ((bf16[32,256,128]{2,1,0:T(8,128)(2,1)}), bf16[32,256,128]{2,1,0:T(8,128)(2,1)}, u32[]{:S(2)}, u32[]{:S(2)}) async-start(bf16[32,256,128]{2,1,0:T(8,128)(2,1)} %filterbank_late.1), calls=%async_computation | async-start | bytes 4194304 | tf_op jit(solution)/shard_map/all_to_all | solution.py:438
  74.1 36.7 %all-to-all-start.2 = ((bf16[32,160,128]{2,1,0:T(8,128)(2,1)}), bf16[32,160,128]{2,1,0:T(8,128)(2,1)S(1)}, u32[]{:S(2)}, u32[]{:S(2)}) async-start(bf16[32,160,128]{2,1,0:T(8,128)(2,1)} %get-tuple-element.18), calls=%async_computation.2 | async-start | bytes 2621440 | tf_op jit(solution)/shard_map/all_to_all | solution.py:457
  110.7 3.9 %copy-start = (bf16[32,160,128]{2,1,0:T(8,128)(2,1)}, bf16[32,160,128]{2,1,0:T(8,128)(2,1)S(1)}, u32[]{:S(2)}) copy-start(bf16[32,160,128]{2,1,0:T(8,128)(2,1)S(1)} %all-to-all-done.2.refs_1_) | copy-start | bytes 3932164
  110.8 24.4 %all-to-all-start.1 = ((bf16[32,96,128]{2,1,0:T(8,128)(2,1)}), bf16[32,96,128]{2,1,0:T(8,128)(2,1)}, u32[]{:S(2)}, u32[]{:S(2)}) async-start(bf16[32,96,128]{2,1,0:T(8,128)(2,1)} %get-tuple-element.17), calls=%async_computation.1 | async-start | bytes 1572864 | tf_op jit(solution)/shard_map/all_to_all | solution.py:460

commit v5 on v4

--- a/solution.py
+++ b/solution.py
@@ -70,13 +70,14 @@
     row_ref, w_ref, c1_ref, cos_ref, sin_ref, w2_ref, results, y_ref, t_ref, d_ref, sems, *outs = refs
 
     def filter_a(taps_of, a, carry):
-        weights = [w_ref[k : k + 1, pl.ds(pl.multiple_of(a * FRAME_B, FRAME_B), FRAME_B)] for k in range(TAPS)]
+        at = pl.multiple_of(a * FRAME_B, FRAME_B)
+        weights = [w_ref[k : k + 1, pl.ds(at, FRAME_B)].astype(jnp.bfloat16) for k in range(TAPS)]
         frames = [taps_of(i, a) for i in range(BATCH + LEAD)]
         for t in range(BATCH):
             total = frames[t] * weights[0]
             for k in range(1, TAPS):
                 total = total + frames[t + k] * weights[k]
-            y_ref[t, pl.ds(pl.multiple_of(a * GROUP, GROUP), GROUP), :] = total.astype(jnp.bfloat16)
+            y_ref[t, pl.ds(pl.multiple_of(a * GROUP, GROUP), GROUP), :] = total
         return carry
 
     if len(sources) == 1:
@@ -164,7 +165,7 @@
 
     def taps_of(i, a):
         at = pl.multiple_of(i * NFFT + a * FRAME_B, FRAME_B)
-        return x_ref[:, pl.ds(at, FRAME_B)].astype(jnp.float32)
+        return x_ref[:, pl.ds(at, FRAME_B)]
 
     refs = (row_ref, w_ref, c1_ref, cos_ref, sin_ref, w2_ref, results, *scratch)
     filterbank_body([taps_of], pl.program_id(0), refs)
@@ -180,7 +181,7 @@
         def taps_of(i, a):
             source, at = (x_ref, i - LEAD) if i >= LEAD else (ahead_ref, i)
             at = pl.multiple_of(at * NFFT + a * FRAME_B, FRAME_B)
-            return source[:, pl.ds(at, FRAME_B)].astype(jnp.float32)
+            return source[:, pl.ds(at, FRAME_B)]
 
         return taps_of
 

time: 147 us -> 146 us (level)
  Pallas kernels: 63.6 us -> 61.6 us
    pallas_call x2, Pallas kernels: 25.9 us -> 23.8 us  [filterbank(): pl.pallas_call(kernel, out_shape=outs, grid_spec=pltpu.PrefetchScalarGrid...]
  transfers between devices with their start and end apart: 4 -> 4, of which waited for: 3 -> 3; matrix products, arithmetic and copies ran while one was open for 1% -> 1% of each run, Pallas kernels for 36% -> 35%
where the time goes in v5:
time: 146 us; the launch traced here: 145 us
  Pallas kernels  61.6 us (42%)
  waiting for transfers between devices  60.8 us (42%)
  starting transfers between devices  18.4 us (13%)
  local copies, waits for them, and re-layouts  2.61 us (2%)
  other arithmetic  1.66 us (1%)
    all_to_all x1, waiting for transfers between devices, fused_body(): late = exchange(late[0])  35 us
    pallas_call x2, Pallas kernels, correlate(): pl.pallas_call(functools.partial(correlate_kernel, scale, sizes, start),...  28.9 us
    pallas_call x2, Pallas kernels, filterbank(): pl.pallas_call(kernel, out_shape=outs, grid_spec=pltpu.PrefetchScalarGrid...  23.8 us
    all_to_all x1, waiting for transfers between devices, fused_body(): early = exchange(early)  23 us
    pallas_call x1, Pallas kernels, order_late(): pl.pallas_call(functools.partial(order_kernel, sizes), out_shape=jax.Shap...  8.85 us
    all_to_all x1, starting transfers between devices, fused_body(): late = exchange(late[0])  5.88 us
    all_to_all x1, starting transfers between devices, fused_body(): early = exchange(early)  4.62 us
    ppermute x1, starting transfers between devices, fused_body(): halo = lax.ppermute(ending, 'tm', [(i, i + 1) for i in range(tm_count - 1)])  3.99 us
  transfers between devices with their start and end apart: 4, of which 3 were waited for; matrix products, arithmetic and copies ran while one was open for 1% of the time, Pallas kernels for 35%

profile of v5, /device:TPU:0, one launch (start us, length us, event | category | flops | bytes accessed | tf_op | source)
XLA Modules:
  0.0 145.3 jit_solution(17883653420435397572)
XLA Ops:
  0.0 2.1 %constant_dynamic-slice_fusion = bf16[64,24576]{1,0:T(8,128)(2,1)S(1)} fusion(bf16[128,65536]{1,0:T(8,128)(2,1)} %x_ref.3, s32[]{:T(128)S(6)} %select_n.42), kind=kLoop, calls=%fused_computation.27 | loop fusion | bytes 6291460 | tf_op jit(solution)/shard_map/dynamic_slice | solution.py:413
  2.1 4.0 %collective-permute-start = (bf16[64,24576]{1,0:T(8,128)(2,1)S(1)}, bf16[64,24576]{1,0:T(8,128)(2,1)}, u32[]{:S(2)}, u32[]{:S(2)}) collective-permute-start(bf16[64,24576]{1,0:T(8,128)(2,1)S(1)} %constant_dynamic-slice_fusion), channel_id=1, source_target_pairs={{0,2},{2,4},{4,6},{1,3},{3,5},{5,7},{8,10},{10,12},{12,14},{9,11},... | collective-permute-start | bytes 9437192 | tf_op jit(solution)/shard_map/ppermute | solution.py:416
  6.1 0.0 copy-done.1
  6.1 0.6 select_select_fusion.row_ref
  6.7 11.8 %filterbank_late.1 = bf16[32,256,128]{2,1,0:T(8,128)(2,1)} custom-call(s32[2050]{0:T(1024)} %select_select_fusion.row_ref, bf16[128,65536]{1,0:T(8,128)(2,1)} %x_ref.3, f32[4,8192]{1,0:T(4,128)} %constant.78.clone.w_ref, bf16[512,512]{1,0:T(8,128)(2,1)} %constant.79.clone.c1_ref, f32[17,256]{1,0:T(8,128)} %constant.80.clone.cos_ref, ...), custom_call_target="tpu_custom_call" | custom-call | flops 12000000000 | bytes 16777216 | tf_op jit(solution)/shard_map/filterbank_late/pallas_call | solution.py:195
  18.5 0.0 copy-start.3
  18.5 0.0 copy-start.2
  18.5 5.9 %all-to-all-start = ((bf16[32,256,128]{2,1,0:T(8,128)(2,1)}), bf16[32,256,128]{2,1,0:T(8,128)(2,1)}, u32[]{:S(2)}, u32[]{:S(2)}) async-start(bf16[32,256,128]{2,1,0:T(8,128)(2,1)} %filterbank_late.1), calls=%async_computation | async-start | bytes 4194304 | tf_op jit(solution)/shard_map/all_to_all | solution.py:439
  24.4 0.0 copy-done.3
  24.4 0.1 broadcast_in_dim.27
  24.6 0.2 eq.38
  24.7 0.1 broadcast_in_dim.26
  24.8 0.1 mul.38
  25.0 1.0 fusion.1.perm_ref.refs_2_
  26.0 0.0 collective-permute-done.halo_ref
  26.0 12.1 %filterbank_early.1 = (bf16[32,160,128]{2,1,0:T(8,128)(2,1)}, bf16[32,96,128]{2,1,0:T(8,128)(2,1)}) custom-call(s32[2050]{0:T(1024)} %select_select_fusion.row_ref, bf16[128,65536]{1,0:T(8,128)(2,1)} %x_ref.3, bf16[64,24576]{1,0:T(8,128)(2,1)} %collective-permute-done.halo_ref, bf16[128,24576]{1,0:T(8,128)(2,1)} %history_ref.1, ...), custom_call_target="tpu_custom_call" | custom-call | flops 12000000000 | bytes 16777216 | tf_op jit(solution)/shard_map/filterbank_early/pallas_call | solution.py:195
  38.1 35.0 %all-to-all-done.late_ref = bf16[32,256,128]{2,1,0:T(8,128)(2,1)} async-done(((bf16[32,256,128]{2,1,0:T(8,128)(2,1)}), bf16[32,256,128]{2,1,0:T(8,128)(2,1)}, u32[]{:S(2)}, u32[]{:S(2)}) %all-to-all-start) | async-done | bytes 2097184 | tf_op jit(solution)/shard_map/all_to_all | solution.py:439
  73.1 4.6 %all-to-all-start.2 = ((bf16[32,160,128]{2,1,0:T(8,128)(2,1)}), bf16[32,160,128]{2,1,0:T(8,128)(2,1)S(1)}, u32[]{:S(2)}, u32[]{:S(2)}) async-start(bf16[32,160,128]{2,1,0:T(8,128)(2,1)} %get-tuple-element.18), calls=%async_computation.2 | async-start | bytes 2621440 | tf_op jit(solution)/shard_map/all_to_all | solution.py:458
  77.8 8.8 %order_late.1.refs_0_ = bf16[64,32,512]{2,1,0:T(8,128)(2,1)} custom-call(bf16[32,256,128]{2,1,0:T(8,128)(2,1)} %all-to-all-done.late_ref, bf16[512,512]{1,0:T(8,128)(2,1)} %fusion.1.perm_ref.refs_2_), custom_call_target="tpu_custom_call" | custom-call | flops 8000000000 | bytes 4194304 | tf_op jit(solution)/shard_map/order_late/pallas_call | solution.py:268
  86.6 23.0 %all-to-all-done.2.refs_1_ = bf16[32,160,128]{2,1,0:T(8,128)(2,1)S(1)} async-done(((bf16[32,160,128]{2,1,0:T(8,128)(2,1)}), bf16[32,160,128]{2,1,0:T(8,128)(2,1)S(1)}, u32[]{:S(2)}, u32[]{:S(2)}) %all-to-all-start.2) | async-done | bytes 1310752 | tf_op jit(solution)/shard_map/all_to_all | solution.py:458
  109.6 3.9 %all-to-all-start.1 = ((bf16[32,96,128]{2,1,0:T(8,128)(2,1)}), bf16[32,96,128]{2,1,0:T(8,128)(2,1)}, u32[]{:S(2)}, u32[]{:S(2)}) async-start(bf16[32,96,128]{2,1,0:T(8,128)(2,1)} %get-tuple-element.17), calls=%async_computation.1 | async-start | bytes 1572864 | tf_op jit(solution)/shard_map/all_to_all | solution.py:461
  113.5 17.7 %correlate.2.refs_3_ = f32[64,512,512]{2,1,0:T(8,128)} custom-call(bf16[64,32,512]{2,1,0:T(8,128)(2,1)} %order_late.1.refs_0_, bf16[32,160,128]{2,1,0:T(8,128)(2,1)} %copy-done, bf16[512,512]{1,0:T(8,128)(2,1)} %fusion.1.perm_ref.refs_2_), custom_call_target="tpu_custom_call" | custom-call | flops 4800000000 | bytes 41943040 | tf_op jit(solution)/shard_map/correlate/pallas_call | solution.py:378
  131.3 2.7 %all-to-all-done.1.refs_1_ = bf16[32,96,128]{2,1,0:T(8,128)(2,1)} async-done(((bf16[32,96,128]{2,1,0:T(8,128)(2,1)}), bf16[32,96,128]{2,1,0:T(8,128)(2,1)}, u32[]{:S(2)}, u32[]{:S(2)}) %all-to-all-start.1) | async-done | bytes 786464 | tf_op jit(solution)/shard_map/all_to_all | solution.py:461
  134.0 11.2 %correlate.3 = f32[64,512,512]{2,1,0:T(8,128)} custom-call(bf16[64,32,512]{2,1,0:T(8,128)(2,1)} %order_late.1.refs_0_, bf16[32,96,128]{2,1,0:T(8,128)(2,1)} %all-to-all-done.1.refs_1_, bf16[512,512]{1,0:T(8,128)(2,1)} %fusion.1.perm_ref.refs_2_, f32[64,512,512]{2,1,0:T(8,128)} %correlate.2.refs_3_), custom_call_target="tpu_custom_call", output_to_operand_aliasing={{}: (3, {})} | custom-call | flops 2880000000 | bytes 25165824 | tf_op jit(solution)/shard_map/correlate/pallas_call | solution.py:378
  (8 shorter events, 0.0 us)
Async XLA Ops:
  0.0 6.1 %copy-start.1 = (s32[2048]{0:T(1024)S(1)}, s32[2048]{0:T(1024)}, u32[]{:S(2)}) copy-start(s32[2048]{0:T(1024)} %param.13) | copy-start | bytes 24580
  2.1 23.9 %collective-permute-start = (bf16[64,24576]{1,0:T(8,128)(2,1)S(1)}, bf16[64,24576]{1,0:T(8,128)(2,1)}, u32[]{:S(2)}, u32[]{:S(2)}) collective-permute-start(bf16[64,24576]{1,0:T(8,128)(2,1)S(1)} %constant_dynamic-slice_fusion), channel_id=1, source_target_pairs={{0,2},{2,4},{4,6},{1,3},{3,5},{5,7},{8,10},{10,12},{12,14},{9,11},... | collective-permute-start | bytes 9437192 | tf_op jit(solution)/shard_map/ppermute | solution.py:416
  18.5 5.9 %copy-start.3 = (s32[256]{0:T(256)S(1)}, s32[256]{0:T(256)}, u32[]{:S(2)}) copy-start(s32[256]{0:T(256)} %param.14) | copy-start | bytes 3076
  18.5 6.2 %copy-start.2 = (s32[256]{0:T(256)S(1)}, s32[256]{0:T(256)}, u32[]{:S(2)}) copy-start(s32[256]{0:T(256)} %param.12) | copy-start | bytes 3076
  18.5 54.6 %all-to-all-start = ((bf16[32,256,128]{2,1,0:T(8,128)(2,1)}), bf16[32,256,128]{2,1,0:T(8,128)(2,1)}, u32[]{:S(2)}, u32[]{:S(2)}) async-start(bf16[32,256,128]{2,1,0:T(8,128)(2,1)} %filterbank_late.1), calls=%async_computation | async-start | bytes 4194304 | tf_op jit(solution)/shard_map/all_to_all | solution.py:439
  73.1 36.5 %all-to-all-start.2 = ((bf16[32,160,128]{2,1,0:T(8,128)(2,1)}), bf16[32,160,128]{2,1,0:T(8,128)(2,1)S(1)}, u32[]{:S(2)}, u32[]{:S(2)}) async-start(bf16[32,160,128]{2,1,0:T(8,128)(2,1)} %get-tuple-element.18), calls=%async_computation.2 | async-start | bytes 2621440 | tf_op jit(solution)/shard_map/all_to_all | solution.py:458
  109.6 3.9 %copy-start = (bf16[32,160,128]{2,1,0:T(8,128)(2,1)}, bf16[32,160,128]{2,1,0:T(8,128)(2,1)S(1)}, u32[]{:S(2)}) copy-start(bf16[32,160,128]{2,1,0:T(8,128)(2,1)S(1)} %all-to-all-done.2.refs_1_) | copy-start | bytes 3932164
  109.6 24.4 %all-to-all-start.1 = ((bf16[32,96,128]{2,1,0:T(8,128)(2,1)}), bf16[32,96,128]{2,1,0:T(8,128)(2,1)}, u32[]{:S(2)}, u32[]{:S(2)}) async-start(bf16[32,96,128]{2,1,0:T(8,128)(2,1)} %get-tuple-element.17), calls=%async_computation.1 | async-start | bytes 1572864 | tf_op jit(solution)/shard_map/all_to_all | solution.py:461
